TPU v7x, 256 devices: a whole 4x4x8 slice. The times are simulated.
256 devices in a mesh: blk: 16 (over z, core), pair: 2 (over x_hi), head: 8 (over y, x_lo).
Axes of the slice: x: 4 (x_hi: 2, x_lo: 2; x = x_hi * 2 + x_lo), y: 4, z: 8, core: 2. Of those that a mesh axis runs over, the one named last changes fastest.
Arguments:
- prefix_query_rows: bfloat16 [2048, 8, 8, 128], P('blk', 'head', 'pair'), may hold values from -6 to 6
- prefix_key_rows: bfloat16 [2048, 8, 128], P('blk', 'head'), may hold values from -6 to 6
- prefix_value_rows: bfloat16 [2048, 8, 128], P('blk', 'head'), may hold values from -6 to 6
- prefix_output_gradient: bfloat16 [2048, 8, 8, 128], P('blk', 'head', 'pair'), may hold values from -6 to 6
- resp_q: bfloat16 [2, 2048, 8, 8, 128], P('pair', 'blk', 'head'), may hold values from -100 to 100
- resp_k: bfloat16 [2, 2048, 8, 128], P('pair', 'blk', 'head'), may hold values from -4 to 4
- response_value_rows: bfloat16 [2, 2048, 8, 128], P('pair', 'blk', 'head'), may hold values from -6 to 6
- response_output_gradient: bfloat16 [2, 2048, 8, 8, 128], P('pair', 'blk', 'head'), may hold values from -6 to 6
- lengths: int32 [2], replicated, may hold values from 128 to 2048, as said below
- prefix_order: int32 [16], replicated, may hold values from 0 to 15, each once
Outputs:
- dprefix_q: bfloat16 [2048, 8, 8, 128], P(('blk', 'head'), None, 'pair')
- dprefix_k: bfloat16 [2048, 8, 128], P(('blk', 'head'))
- dprefix_v: bfloat16 [2048, 8, 128], P(('blk', 'head'))
- dresp_q: bfloat16 [2, 2048, 8, 8, 128], P('pair', ('blk', 'head'))
- dresp_k: bfloat16 [2, 2048, 8, 128], P('pair', ('blk', 'head'))
- dresp_v: bfloat16 [2, 2048, 8, 128], P('pair', ('blk', 'head'))
Inputs may be any that keep to these rules, and one draw needn't show every extreme that they name: `prefix_order`: the stored prefix blocks are the prefix blocks 0 to 15, each once. Each length is a multiple of 128; one of the two lengths equals 2048.
All inputs are finite; a program needn't handle non-finite values.
Results may differ from a plain program's by a relative error of at most 0.0051.
Values may be sent and summed in bfloat16 or wider, within the bound.
A program may use at most 128 MiB of HBM per device.

v0:
```python
import jax
import jax.numpy as jnp
from jax import lax
from jax.sharding import PartitionSpec as P

PBLK = 128


very_low = -1e30


def shifted(value, axis, steps):
    count = lax.axis_size(axis)
    pairs = [(source, (source + steps) % count) for source in range(count)]
    return lax.ppermute(value, axis, pairs)


def on_device(
    prefix_query_rows,
    prefix_key_rows,
    prefix_value_rows,
    prefix_output_gradient,
    resp_q,
    resp_k,
    response_value_rows,
    response_output_gradient,
    lengths,
    prefix_order,
):
    cycle_size = lax.axis_size("blk")
    cycle_index = lax.axis_index("blk")
    pair_index = lax.axis_index("pair")
    pref_rows = prefix_key_rows.shape[0]
    local_heads = prefix_key_rows.shape[1]
    head_size = prefix_key_rows.shape[2]
    half_heads = prefix_query_rows.shape[2]
    resp_rows = resp_k.shape[1]
    all_heads = resp_q.shape[3]
    block_rows = pref_rows + resp_rows
    prefix_total = pref_rows * cycle_size
    scaling = head_size ** (-0.5)
    slot_table = jnp.arange(prefix_order.shape[0], dtype=jnp.int32)

    def key_positions(begin_row, row_count):
        row_index = begin_row + jnp.arange(row_count, dtype=jnp.int32)
        owners = row_index // block_rows
        offset = row_index % block_rows
        slot_ids = owners * (pref_rows // PBLK) + jnp.minimum(offset, pref_rows - 1) // PBLK
        chosen = jnp.sum(
            jnp.where(slot_ids[:, None] == slot_table[None, :], prefix_order[None, :], 0), axis=1
        )
        prefix_pos = chosen * PBLK + offset % PBLK
        resp_pos = prefix_total + owners * resp_rows + offset - pref_rows
        return jnp.where(offset < pref_rows, prefix_pos, resp_pos)

    own_prefix = key_positions(cycle_index * block_rows, pref_rows)
    own_resp = prefix_total + cycle_index * resp_rows + jnp.arange(resp_rows, dtype=jnp.int32)
    query_pos = jnp.concatenate(
        [jnp.repeat(own_prefix, half_heads), jnp.repeat(own_resp, all_heads)]
    )
    live_len = jnp.sum(jnp.where(jnp.arange(2) == pair_index, lengths, 0))
    live_rows = own_resp - prefix_total < live_len
    resp_douts = jnp.where(
        live_rows[:, None, None, None], response_output_gradient[0], jnp.zeros((), jnp.bfloat16)
    )
    queries = jnp.concatenate(
        [
            prefix_query_rows.transpose(1, 0, 2, 3).reshape(local_heads, -1, head_size),
            resp_q[0].transpose(1, 0, 2, 3).reshape(local_heads, -1, head_size),
        ],
        axis=1,
    )
    grad_outs = jnp.concatenate(
        [
            prefix_output_gradient.transpose(1, 0, 2, 3).reshape(local_heads, -1, head_size),
            resp_douts.transpose(1, 0, 2, 3).reshape(local_heads, -1, head_size),
        ],
        axis=1,
    )
    key_value = jnp.stack(
        [
            jnp.concatenate([prefix_key_rows, resp_k[0]], axis=0),
            jnp.concatenate([prefix_value_rows, response_value_rows[0]], axis=0),
        ]
    ).transpose(0, 2, 1, 3)
    query_rows = queries.shape[1]

    def scores_of(pieces, begin_row):
        visible = (
            key_positions(begin_row, pieces.shape[2])[None, None, :] <= query_pos[None, :, None]
        )
        logits = (
            jnp.einsum("gqd,gkd->gqk", queries, pieces[0], preferred_element_type=jnp.float32)
            * scaling
        )
        dprobs = jnp.einsum(
            "gqd,gkd->gqk", grad_outs, pieces[1], preferred_element_type=jnp.float32
        )
        return (logits, dprobs, visible)

    running_max = jnp.full((local_heads, query_rows), very_low, jnp.float32)
    logits, dprobs, visible = scores_of(
        lax.all_gather(key_value, "blk", axis=2, tiled=True), jnp.int32(0)
    )
    new_max = jnp.maximum(running_max, jnp.max(jnp.where(visible, logits, very_low), axis=2))
    weights = jnp.where(visible, jnp.exp(logits - new_max[:, :, None]), 0.0)
    running_sum = jnp.sum(weights, axis=2)
    running_dot = jnp.sum(weights * dprobs, axis=2)
    log_total = new_max + jnp.log(running_sum)
    deltas = running_dot / running_sum

    def grad_terms(pieces, begin_row):
        logits, dprobs, visible = scores_of(pieces, begin_row)
        softmax = jnp.where(visible, jnp.exp(logits - log_total[:, :, None]), 0.0)
        dscores = (softmax * (dprobs - deltas[:, :, None]) * scaling).astype(jnp.bfloat16)
        soft_bf = softmax.astype(jnp.bfloat16)
        dq_term = jnp.einsum("gqk,gkd->gqd", dscores, pieces[0], preferred_element_type=jnp.float32)
        dk_term = jnp.einsum("gqk,gqd->gkd", dscores, queries, preferred_element_type=jnp.float32)
        dv_term = jnp.einsum("gqk,gqd->gkd", soft_bf, grad_outs, preferred_element_type=jnp.float32)
        return (dq_term, jnp.stack([dk_term, dv_term]))

    dq_sum, grads_held = grad_terms(key_value, cycle_index * block_rows)

    def back_turn(cycle_state, cycle_step):
        blocks_held, grads_held, dq_sum = cycle_state
        blocks_held = shifted(blocks_held, "blk", 1)
        grads_held = shifted(grads_held, "blk", 1)
        owners = (cycle_index - cycle_step) % cycle_size
        dq_term, kv_term = grad_terms(blocks_held, owners * block_rows)
        return ((blocks_held, grads_held + kv_term, dq_sum + dq_term), None)

    final_state, unused = lax.scan(
        back_turn, (key_value, grads_held, dq_sum), jnp.arange(1, cycle_size, dtype=jnp.int32)
    )
    grads_final = final_state[1]
    dq_sum = final_state[2]
    kv_grads = shifted(grads_final, "blk", 1)
    split_row = pref_rows * half_heads
    dq_pref = (
        dq_sum[:, :split_row]
        .reshape(local_heads, pref_rows, half_heads, head_size)
        .transpose(1, 0, 2, 3)
        .astype(jnp.bfloat16)
    )
    dq_resp = (
        dq_sum[:, split_row:]
        .reshape(local_heads, resp_rows, all_heads, head_size)
        .transpose(1, 0, 2, 3)
        .astype(jnp.bfloat16)
    )
    pref_grads = kv_grads[:, :, :pref_rows].transpose(0, 2, 1, 3)
    resp_grads = kv_grads[:, :, pref_rows:].transpose(0, 2, 1, 3).astype(jnp.bfloat16)
    summed = lax.psum(pref_grads, "pair").astype(jnp.bfloat16)
    prefix_dq, prefix_dk, prefix_dv, resp_dq, resp_dk, resp_dv = (
        lax.all_to_all(dq_pref, "head", split_axis=0, concat_axis=1, tiled=True),
        lax.all_to_all(summed[0], "head", split_axis=0, concat_axis=1, tiled=True),
        lax.all_to_all(summed[1], "head", split_axis=0, concat_axis=1, tiled=True),
        lax.all_to_all(dq_resp, "head", split_axis=0, concat_axis=1, tiled=True),
        lax.all_to_all(resp_grads[0], "head", split_axis=0, concat_axis=1, tiled=True),
        lax.all_to_all(resp_grads[1], "head", split_axis=0, concat_axis=1, tiled=True),
    )
    return (prefix_dq, prefix_dk, prefix_dv, resp_dq[None], resp_dk[None], resp_dv[None])


def solution(mesh):
    in_specs = (
        P("blk", "head", "pair", None),
        P("blk", "head", None),
        P("blk", "head", None),
        P("blk", "head", "pair", None),
        P("pair", "blk", "head", None, None),
        P("pair", "blk", "head", None),
        P("pair", "blk", "head", None),
        P("pair", "blk", "head", None, None),
        P(),
        P(),
    )
    out_specs = (
        P(("blk", "head"), None, "pair", None),
        P(("blk", "head"), None, None),
        P(("blk", "head"), None, None),
        P("pair", ("blk", "head"), None, None, None),
        P("pair", ("blk", "head"), None, None),
        P("pair", ("blk", "head"), None, None),
    )
    return jax.shard_map(
        on_device, mesh=mesh, in_specs=in_specs, out_specs=out_specs, check_vma=False
    )
```

profile of v0, /device:TPU:2, one launch (start us, length us, event | category | flops | bytes accessed | tf_op | source)
XLA Modules:
  0.0 297.2 jit_solution(5958794377940642063)
XLA Ops:
  7.2 0.9 fusion.37
  8.1 0.7 pad_maximum_fusion.3
  8.9 0.7 select_reduce_fusion.3
  10.0 1.3 fusion.62
  12.3 0.7 select_reduce_fusion.2
  13.0 0.8 select_reduce_fusion.1
  13.8 1.2 bitcast_select_fusion
  15.1 38.1 %all-gather.3.cloned.1.call-done = bf16[2,4096,1,128]{3,1,0,2:T(8,128)(2,1)} async-done(((bf16[2,256,1,128]{3,1,0,2:T(8,128)(2,1)}), bf16[2,4096,1,128]{3,1,0,2:T(8,128)(2,1)}) %all-gather.3.cloned.1.call-update) | async-done | bytes 2097168 | tf_op jit(solution)/shard_map/all_gather | solution.py:103
  53.2 12.2 %fusion.18 = (f32[1536]{0:T(1024)S(1)}, f32[1536,4096]{1,0:T(8,128)}) fusion(s32[4096]{0:T(1024)S(1)} %fusion.45, s32[1536]{0:T(1024)S(1)} %constant_dynamic-update-slice_fusion, bf16[2,4096,1,128]{3,1,0,2:T(8,128)(2,1)} %all-gather.3.cloned.1.call-done, bf16[1,1024,128]{2,1,0:T(8,128)(2,1)S(1)} %bitcast.165, bf16[1,512,128]{2,1,0:T(8,128)(2,1)S(1)} %bitcast.171), kind=kOutput, calls=%fused_computation.44 | convolution fusion | flops 1636563456 | bytes 26636288 | tf_op jit(solution)/shard_map/gqd,gkd->gqk/dot_general | solution.py:93
  65.4 11.9 %fusion.19 = f32[1536]{0:T(1024)S(1)} fusion(f32[1536,4096]{1,0:T(8,128)} %get-tuple-element.316, f32[1536]{0:T(1024)S(1)} %broadcast_maximum_fusion, s32[4096]{0:T(1024)S(1)} %fusion.45, s32[1536]{0:T(1024)S(1)} %constant_dynamic-update-slice_fusion), kind=kLoop, calls=%fused_computation.46 | loop fusion | flops 31455744 | bytes 25200640 | tf_op jit(solution)/shard_map/reduce_sum | solution.py:107
  77.4 13.1 %multiply_reduce_fusion = f32[1536]{0:T(1024)S(1)} fusion(f32[1536,4096]{1,0:T(8,128)} %get-tuple-element.316, f32[1536]{0:T(1024)S(1)} %broadcast_maximum_fusion, s32[4096]{0:T(1024)S(1)} %fusion.45, s32[1536]{0:T(1024)S(1)} %constant_dynamic-update-slice_fusion, bf16[2,4096,1,128]{3,1,0,2:T(8,128)(2,1)S(1)} %copy-done.8, ...), kind=kOutput, calls=%fused_computation.45 | convolution fusion | flops 1649146368 | bytes 26646528 | tf_op jit(solution)/shard_map/gqd,gkd->gqk/dot_general | solution.py:96
  93.1 127.2 %while.18 = (s32[]{:T(128)}, bf16[2,1,256,128]{3,2,1,0:T(8,128)(2,1)S(1)}, f32[2,1,256,128]{3,2,1,0:T(8,128)S(1)}, f32[1,1536,128]{2,1,0:T(8,128)S(1)}, s32[15]{...) while((s32[]{:T(128)}, ...), condition=%wide.region_9.10_spmd.clone, body=%wide.region_7.9_spmd.clone.sunk | while | flops 507214592 | bytes 13359574 | solution.py:132
  93.4 0.7 collective-permute-start.1
  95.5 3.2 %collective-permute-done = bf16[2,1,256,128]{3,2,1,0:T(8,128)(2,1)S(1)} collective-permute-done((bf16[2,1,256,128]{3,2,1,0:T(8,128)(2,1)S(1)}, bf16[2,1,256,128]{3,2,1,0:T(8,128)(2,1)S(1)}, u32[]{:S(2)}, u32[]{:S(2)}) %collective-permute-start) | collective-permute-done | bytes 131104 | tf_op jit(solution)/shard_map/while/body/eval_jaxpr/ppermute | solution.py:15
  103.1 4.1 %collective-permute-done = bf16[2,1,256,128]{3,2,1,0:T(8,128)(2,1)S(1)} collective-permute-done((bf16[2,1,256,128]{3,2,1,0:T(8,128)(2,1)S(1)}, bf16[2,1,256,128]{3,2,1,0:T(8,128)(2,1)S(1)}, u32[]{:S(2)}, u32[]{:S(2)}) %collective-permute-start) | collective-permute-done | bytes 131104 | tf_op jit(solution)/shard_map/while/body/eval_jaxpr/ppermute | solution.py:15
  111.6 4.1 %collective-permute-done = bf16[2,1,256,128]{3,2,1,0:T(8,128)(2,1)S(1)} collective-permute-done((bf16[2,1,256,128]{3,2,1,0:T(8,128)(2,1)S(1)}, bf16[2,1,256,128]{3,2,1,0:T(8,128)(2,1)S(1)}, u32[]{:S(2)}, u32[]{:S(2)}) %collective-permute-start) | collective-permute-done | bytes 131104 | tf_op jit(solution)/shard_map/while/body/eval_jaxpr/ppermute | solution.py:15
  120.1 4.1 %collective-permute-done = bf16[2,1,256,128]{3,2,1,0:T(8,128)(2,1)S(1)} collective-permute-done((bf16[2,1,256,128]{3,2,1,0:T(8,128)(2,1)S(1)}, bf16[2,1,256,128]{3,2,1,0:T(8,128)(2,1)S(1)}, u32[]{:S(2)}, u32[]{:S(2)}) %collective-permute-start) | collective-permute-done | bytes 131104 | tf_op jit(solution)/shard_map/while/body/eval_jaxpr/ppermute | solution.py:15
  128.5 4.1 %collective-permute-done = bf16[2,1,256,128]{3,2,1,0:T(8,128)(2,1)S(1)} collective-permute-done((bf16[2,1,256,128]{3,2,1,0:T(8,128)(2,1)S(1)}, bf16[2,1,256,128]{3,2,1,0:T(8,128)(2,1)S(1)}, u32[]{:S(2)}, u32[]{:S(2)}) %collective-permute-start) | collective-permute-done | bytes 131104 | tf_op jit(solution)/shard_map/while/body/eval_jaxpr/ppermute | solution.py:15
  137.0 4.1 %collective-permute-done = bf16[2,1,256,128]{3,2,1,0:T(8,128)(2,1)S(1)} collective-permute-done((bf16[2,1,256,128]{3,2,1,0:T(8,128)(2,1)S(1)}, bf16[2,1,256,128]{3,2,1,0:T(8,128)(2,1)S(1)}, u32[]{:S(2)}, u32[]{:S(2)}) %collective-permute-start) | collective-permute-done | bytes 131104 | tf_op jit(solution)/shard_map/while/body/eval_jaxpr/ppermute | solution.py:15
  145.5 4.1 %collective-permute-done = bf16[2,1,256,128]{3,2,1,0:T(8,128)(2,1)S(1)} collective-permute-done((bf16[2,1,256,128]{3,2,1,0:T(8,128)(2,1)S(1)}, bf16[2,1,256,128]{3,2,1,0:T(8,128)(2,1)S(1)}, u32[]{:S(2)}, u32[]{:S(2)}) %collective-permute-start) | collective-permute-done | bytes 131104 | tf_op jit(solution)/shard_map/while/body/eval_jaxpr/ppermute | solution.py:15
  154.0 4.1 %collective-permute-done = bf16[2,1,256,128]{3,2,1,0:T(8,128)(2,1)S(1)} collective-permute-done((bf16[2,1,256,128]{3,2,1,0:T(8,128)(2,1)S(1)}, bf16[2,1,256,128]{3,2,1,0:T(8,128)(2,1)S(1)}, u32[]{:S(2)}, u32[]{:S(2)}) %collective-permute-start) | collective-permute-done | bytes 131104 | tf_op jit(solution)/shard_map/while/body/eval_jaxpr/ppermute | solution.py:15
  162.5 4.1 %collective-permute-done = bf16[2,1,256,128]{3,2,1,0:T(8,128)(2,1)S(1)} collective-permute-done((bf16[2,1,256,128]{3,2,1,0:T(8,128)(2,1)S(1)}, bf16[2,1,256,128]{3,2,1,0:T(8,128)(2,1)S(1)}, u32[]{:S(2)}, u32[]{:S(2)}) %collective-permute-start) | collective-permute-done | bytes 131104 | tf_op jit(solution)/shard_map/while/body/eval_jaxpr/ppermute | solution.py:15
  170.9 4.1 %collective-permute-done = bf16[2,1,256,128]{3,2,1,0:T(8,128)(2,1)S(1)} collective-permute-done((bf16[2,1,256,128]{3,2,1,0:T(8,128)(2,1)S(1)}, bf16[2,1,256,128]{3,2,1,0:T(8,128)(2,1)S(1)}, u32[]{:S(2)}, u32[]{:S(2)}) %collective-permute-start) | collective-permute-done | bytes 131104 | tf_op jit(solution)/shard_map/while/body/eval_jaxpr/ppermute | solution.py:15
  179.4 4.1 %collective-permute-done = bf16[2,1,256,128]{3,2,1,0:T(8,128)(2,1)S(1)} collective-permute-done((bf16[2,1,256,128]{3,2,1,0:T(8,128)(2,1)S(1)}, bf16[2,1,256,128]{3,2,1,0:T(8,128)(2,1)S(1)}, u32[]{:S(2)}, u32[]{:S(2)}) %collective-permute-start) | collective-permute-done | bytes 131104 | tf_op jit(solution)/shard_map/while/body/eval_jaxpr/ppermute | solution.py:15
  187.9 4.1 %collective-permute-done = bf16[2,1,256,128]{3,2,1,0:T(8,128)(2,1)S(1)} collective-permute-done((bf16[2,1,256,128]{3,2,1,0:T(8,128)(2,1)S(1)}, bf16[2,1,256,128]{3,2,1,0:T(8,128)(2,1)S(1)}, u32[]{:S(2)}, u32[]{:S(2)}) %collective-permute-start) | collective-permute-done | bytes 131104 | tf_op jit(solution)/shard_map/while/body/eval_jaxpr/ppermute | solution.py:15
  196.4 4.1 %collective-permute-done = bf16[2,1,256,128]{3,2,1,0:T(8,128)(2,1)S(1)} collective-permute-done((bf16[2,1,256,128]{3,2,1,0:T(8,128)(2,1)S(1)}, bf16[2,1,256,128]{3,2,1,0:T(8,128)(2,1)S(1)}, u32[]{:S(2)}, u32[]{:S(2)}) %collective-permute-start) | collective-permute-done | bytes 131104 | tf_op jit(solution)/shard_map/while/body/eval_jaxpr/ppermute | solution.py:15
  204.9 4.1 %collective-permute-done = bf16[2,1,256,128]{3,2,1,0:T(8,128)(2,1)S(1)} collective-permute-done((bf16[2,1,256,128]{3,2,1,0:T(8,128)(2,1)S(1)}, bf16[2,1,256,128]{3,2,1,0:T(8,128)(2,1)S(1)}, u32[]{:S(2)}, u32[]{:S(2)}) %collective-permute-start) | collective-permute-done | bytes 131104 | tf_op jit(solution)/shard_map/while/body/eval_jaxpr/ppermute | solution.py:15
  213.3 4.1 %collective-permute-done = bf16[2,1,256,128]{3,2,1,0:T(8,128)(2,1)S(1)} collective-permute-done((bf16[2,1,256,128]{3,2,1,0:T(8,128)(2,1)S(1)}, bf16[2,1,256,128]{3,2,1,0:T(8,128)(2,1)S(1)}, u32[]{:S(2)}, u32[]{:S(2)}) %collective-permute-start) | collective-permute-done | bytes 131104 | tf_op jit(solution)/shard_map/while/body/eval_jaxpr/ppermute | solution.py:15
  220.4 0.7 slice.72
  221.1 5.7 %all-to-all-start = ((bf16[128,1,4,128]{3,2,1,0:T(4,128)(2,1)}), bf16[128,1,4,128]{3,2,1,0:T(4,128)(2,1)S(1)}, u32[]{:S(2)}, u32[]{:S(2)}) async-start(bf16[128,1,4,128]{3,2,1,0:T(4,128)(2,1)} %bitcast.19), calls=%async_computation | async-start | bytes 262144 | tf_op jit(solution)/shard_map/all_to_all | solution.py:155
  226.8 0.7 slice_bitcast_fusion.9
  227.5 4.7 %all-to-all-done = bf16[128,1,4,128]{3,2,1,0:T(4,128)(2,1)S(1)} async-done(((bf16[128,1,4,128]{3,2,1,0:T(4,128)(2,1)}), bf16[128,1,4,128]{3,2,1,0:T(4,128)(2,1)S(1)}, u32[]{:S(2)}, u32[]{:S(2)}) %all-to-all-start) | async-done | bytes 131104 | tf_op jit(solution)/shard_map/all_to_all | solution.py:155
  232.2 4.6 %all-to-all-start.3 = ((bf16[128,1,8,128]{3,2,1,0:T(8,128)(2,1)}), bf16[128,1,8,128]{3,2,1,0:T(8,128)(2,1)S(1)}, u32[]{:S(2)}, u32[]{:S(2)}) async-start(bf16[128,1,8,128]{3,2,1,0:T(8,128)(2,1)} %slice_bitcast_fusion.9), calls=%async_computation.3 | async-start | bytes 524288 | tf_op jit(solution)/shard_map/all_to_all | solution.py:158
  236.8 11.8 %all-reduce.1 = bf16[2,128,1,128]{3,1,2,0:T(8,128)(2,1)S(1)} all-reduce(f32[2,128,1,128]{3,1,2,0:T(8,128)S(1)} %slice_bitcast_fusion.10), channel_id=1, replica_groups=mesh['blk'=16,'pair'=2,'head'=8] {'pair'}, use_global_device_ids=true, to_apply=%region_10.11 | all-reduce | flops 32768 | bytes 196608 | tf_op jit(solution)/shard_map/psum | solution.py:153
  249.1 0.7 reduce.8
  250.4 5.7 %all-to-all-start.1 = ((bf16[8,2,1024]{2,1,0:T(2,128)(2,1)}), bf16[8,2,1024]{2,1,0:T(2,128)(2,1)S(1)}, u32[]{:S(2)}, u32[]{:S(2)}) async-start(bf16[8,2,1024]{2,1,0:T(2,128)(2,1)} %reshape.660), calls=%async_computation.1 | async-start | bytes 65536 | tf_op jit(solution)/shard_map/all_to_all | solution.py:156
  256.2 0.7 reduce.9
  257.5 3.6 %all-to-all-done.1 = bf16[8,2,1024]{2,1,0:T(2,128)(2,1)S(1)} async-done(((bf16[8,2,1024]{2,1,0:T(2,128)(2,1)}), bf16[8,2,1024]{2,1,0:T(2,128)(2,1)S(1)}, u32[]{:S(2)}, u32[]{:S(2)}) %all-to-all-start.1) | async-done | bytes 32800 | tf_op jit(solution)/shard_map/all_to_all | solution.py:156
  261.1 4.6 %all-to-all-start.2 = ((bf16[8,2,1024]{2,1,0:T(2,128)(2,1)}), bf16[8,2,1024]{2,1,0:T(2,128)(2,1)S(1)}, u32[]{:S(2)}, u32[]{:S(2)}) async-start(bf16[8,2,1024]{2,1,0:T(2,128)(2,1)} %reshape.662), calls=%async_computation.2 | async-start | bytes 65536 | tf_op jit(solution)/shard_map/all_to_all | solution.py:157
  265.7 0.7 reduce.10
  267.0 3.6 %all-to-all-done.2 = bf16[8,2,1024]{2,1,0:T(2,128)(2,1)S(1)} async-done(((bf16[8,2,1024]{2,1,0:T(2,128)(2,1)}), bf16[8,2,1024]{2,1,0:T(2,128)(2,1)S(1)}, u32[]{:S(2)}, u32[]{:S(2)}) %all-to-all-start.2) | async-done | bytes 32800 | tf_op jit(solution)/shard_map/all_to_all | solution.py:157
  270.6 4.6 %all-to-all-start.4 = ((bf16[8,2,1024]{2,1,0:T(2,128)(2,1)}), bf16[8,2,1024]{2,1,0:T(2,128)(2,1)S(1)}, u32[]{:S(2)}, u32[]{:S(2)}) async-start(bf16[8,2,1024]{2,1,0:T(2,128)(2,1)} %reshape.664), calls=%async_computation.4 | async-start | bytes 65536 | tf_op jit(solution)/shard_map/all_to_all | solution.py:159
  275.2 0.7 reduce.11
  276.5 3.6 %all-to-all-done.4 = bf16[8,2,1024]{2,1,0:T(2,128)(2,1)S(1)} async-done(((bf16[8,2,1024]{2,1,0:T(2,128)(2,1)}), bf16[8,2,1024]{2,1,0:T(2,128)(2,1)S(1)}, u32[]{:S(2)}, u32[]{:S(2)}) %all-to-all-start.4) | async-done | bytes 32800 | tf_op jit(solution)/shard_map/all_to_all | solution.py:159
  280.1 4.6 %all-to-all-start.5 = ((bf16[8,2,1024]{2,1,0:T(2,128)(2,1)}), bf16[8,2,1024]{2,1,0:T(2,128)(2,1)S(1)}, u32[]{:S(2)}, u32[]{:S(2)}) async-start(bf16[8,2,1024]{2,1,0:T(2,128)(2,1)} %reshape.666), calls=%async_computation.5 | async-start | bytes 65536 | tf_op jit(solution)/shard_map/all_to_all | solution.py:160
  284.8 0.8 copy.66
  285.5 0.8 copy.69
  288.3 1.4 all-to-all-done.5
  (314 shorter events, 64.1 us)
Async XLA Ops:
  7.2 7.8 %copy-start.4 = (bf16[128,1,4,128]{3,2,1,0:T(4,128)(2,1)S(1)}, bf16[128,1,4,128]{3,2,1,0:T(4,128)(2,1)}, u32[]{:S(2)}) copy-start(bf16[128,1,4,128]{3,2,1,0:T(4,128)(2,1)} %param.12) | copy-start | bytes 393220
  7.2 7.8 %copy-start.1 = (bf16[1,128,1,8,128]{4,3,2,1,0:T(8,128)(2,1)S(1)}, bf16[1,128,1,8,128]{4,3,2,1,0:T(8,128)(2,1)}, u32[]{:S(2)}) copy-start(bf16[1,128,1,8,128]{4,3,2,1,0:T(8,128)(2,1)} %param.16) | copy-start | bytes 786436
  7.2 7.8 %copy-start = (bf16[128,1,4,128]{3,2,1,0:T(4,128)(2,1)S(1)}, bf16[128,1,4,128]{3,2,1,0:T(4,128)(2,1)}, u32[]{:S(2)}) copy-start(bf16[128,1,4,128]{3,2,1,0:T(4,128)(2,1)} %param.15) | copy-start | bytes 393220
  7.2 46.0 %all-gather.3.cloned.1.call-start = ((), (), s32[]{:S(2)}) async-start(), calls=%async_computation.6 | async-start | bytes 2228224 | tf_op jit(solution)/shard_map/all_gather | solution.py:103
  65.4 11.9 %copy-start.8 = (bf16[2,4096,1,128]{3,1,0,2:T(8,128)(2,1)S(1)}, bf16[2,4096,1,128]{3,1,0,2:T(8,128)(2,1)}, u32[]{:S(2)}) copy-start(bf16[2,4096,1,128]{3,1,0,2:T(8,128)(2,1)} %all-gather.3.cloned.1.call-done) | copy-start | bytes 6291460
  77.4 13.2 %copy-start.5 = (bf16[1,128,1,128]{3,1,2,0:T(8,128)(2,1)S(1)}, bf16[1,128,1,128]{3,1,2,0:T(8,128)(2,1)}, u32[]{:S(2)}) copy-start(bf16[1,128,1,128]{3,1,2,0:T(8,128)(2,1)} %param.17) | copy-start | bytes 98308
  77.4 13.2 %copy-start.6 = (bf16[128,1,128]{2,0,1:T(8,128)(2,1)S(1)}, bf16[128,1,128]{2,0,1:T(8,128)(2,1)}, u32[]{:S(2)}) copy-start(bf16[128,1,128]{2,0,1:T(8,128)(2,1)} %param.13) | copy-start | bytes 98308
  90.5 0.8 copy-start.2
  90.5 0.8 copy-start.3
  92.5 0.7 copy-start.7
  93.1 5.6 %collective-permute-start = (bf16[2,1,256,128]{3,2,1,0:T(8,128)(2,1)S(1)}, bf16[2,1,256,128]{3,2,1,0:T(8,128)(2,1)S(1)}, u32[]{:S(2)}, u32[]{:S(2)}) collective-permute-start(bf16[2,1,256,128]{3,2,1,0:T(8,128)(2,1)S(1)} %get-tuple-element.413), channel_id=1, source_target_pairs={{0,16},{16,32},{32,48},{48,64},{64,80},{80,96},{96,112},{112,128},... | collective-permute-start | bytes 393224 | tf_op jit(solution)/shard_map/while/body/eval_jaxpr/ppermute | solution.py:15
  93.4 8.2 %collective-permute-start.1 = (f32[2,1,256,128]{3,2,1,0:T(8,128)S(1)}, f32[2,1,256,128]{3,2,1,0:T(8,128)S(1)}, u32[]{:S(2)}, u32[]{:S(2)}) collective-permute-start(f32[2,1,256,128]{3,2,1,0:T(8,128)S(1)} %get-tuple-element.414), channel_id=1, source_target_pairs={{0,16},{16,32},{32,48},{48,64},{64,80},{80,96},{96,112},{112,128},... | collective-permute-start | bytes 786440 | tf_op jit(solution)/shard_map/while/body/eval_jaxpr/ppermute | solution.py:15
  101.6 5.6 %collective-permute-start = (bf16[2,1,256,128]{3,2,1,0:T(8,128)(2,1)S(1)}, bf16[2,1,256,128]{3,2,1,0:T(8,128)(2,1)S(1)}, u32[]{:S(2)}, u32[]{:S(2)}) collective-permute-start(bf16[2,1,256,128]{3,2,1,0:T(8,128)(2,1)S(1)} %get-tuple-element.413), channel_id=1, source_target_pairs={{0,16},{16,32},{32,48},{48,64},{64,80},{80,96},{96,112},{112,128},... | collective-permute-start | bytes 393224 | tf_op jit(solution)/shard_map/while/body/eval_jaxpr/ppermute | solution.py:15
  101.6 8.4 %collective-permute-start.1 = (f32[2,1,256,128]{3,2,1,0:T(8,128)S(1)}, f32[2,1,256,128]{3,2,1,0:T(8,128)S(1)}, u32[]{:S(2)}, u32[]{:S(2)}) collective-permute-start(f32[2,1,256,128]{3,2,1,0:T(8,128)S(1)} %get-tuple-element.414), channel_id=1, source_target_pairs={{0,16},{16,32},{32,48},{48,64},{64,80},{80,96},{96,112},{112,128},... | collective-permute-start | bytes 786440 | tf_op jit(solution)/shard_map/while/body/eval_jaxpr/ppermute | solution.py:15
  110.1 5.6 %collective-permute-start = (bf16[2,1,256,128]{3,2,1,0:T(8,128)(2,1)S(1)}, bf16[2,1,256,128]{3,2,1,0:T(8,128)(2,1)S(1)}, u32[]{:S(2)}, u32[]{:S(2)}) collective-permute-start(bf16[2,1,256,128]{3,2,1,0:T(8,128)(2,1)S(1)} %get-tuple-element.413), channel_id=1, source_target_pairs={{0,16},{16,32},{32,48},{48,64},{64,80},{80,96},{96,112},{112,128},... | collective-permute-start | bytes 393224 | tf_op jit(solution)/shard_map/while/body/eval_jaxpr/ppermute | solution.py:15
  110.1 8.4 %collective-permute-start.1 = (f32[2,1,256,128]{3,2,1,0:T(8,128)S(1)}, f32[2,1,256,128]{3,2,1,0:T(8,128)S(1)}, u32[]{:S(2)}, u32[]{:S(2)}) collective-permute-start(f32[2,1,256,128]{3,2,1,0:T(8,128)S(1)} %get-tuple-element.414), channel_id=1, source_target_pairs={{0,16},{16,32},{32,48},{48,64},{64,80},{80,96},{96,112},{112,128},... | collective-permute-start | bytes 786440 | tf_op jit(solution)/shard_map/while/body/eval_jaxpr/ppermute | solution.py:15
  118.6 5.6 %collective-permute-start = (bf16[2,1,256,128]{3,2,1,0:T(8,128)(2,1)S(1)}, bf16[2,1,256,128]{3,2,1,0:T(8,128)(2,1)S(1)}, u32[]{:S(2)}, u32[]{:S(2)}) collective-permute-start(bf16[2,1,256,128]{3,2,1,0:T(8,128)(2,1)S(1)} %get-tuple-element.413), channel_id=1, source_target_pairs={{0,16},{16,32},{32,48},{48,64},{64,80},{80,96},{96,112},{112,128},... | collective-permute-start | bytes 393224 | tf_op jit(solution)/shard_map/while/body/eval_jaxpr/ppermute | solution.py:15
  118.6 8.4 %collective-permute-start.1 = (f32[2,1,256,128]{3,2,1,0:T(8,128)S(1)}, f32[2,1,256,128]{3,2,1,0:T(8,128)S(1)}, u32[]{:S(2)}, u32[]{:S(2)}) collective-permute-start(f32[2,1,256,128]{3,2,1,0:T(8,128)S(1)} %get-tuple-element.414), channel_id=1, source_target_pairs={{0,16},{16,32},{32,48},{48,64},{64,80},{80,96},{96,112},{112,128},... | collective-permute-start | bytes 786440 | tf_op jit(solution)/shard_map/while/body/eval_jaxpr/ppermute | solution.py:15
  127.0 5.6 %collective-permute-start = (bf16[2,1,256,128]{3,2,1,0:T(8,128)(2,1)S(1)}, bf16[2,1,256,128]{3,2,1,0:T(8,128)(2,1)S(1)}, u32[]{:S(2)}, u32[]{:S(2)}) collective-permute-start(bf16[2,1,256,128]{3,2,1,0:T(8,128)(2,1)S(1)} %get-tuple-element.413), channel_id=1, source_target_pairs={{0,16},{16,32},{32,48},{48,64},{64,80},{80,96},{96,112},{112,128},... | collective-permute-start | bytes 393224 | tf_op jit(solution)/shard_map/while/body/eval_jaxpr/ppermute | solution.py:15
  127.1 8.4 %collective-permute-start.1 = (f32[2,1,256,128]{3,2,1,0:T(8,128)S(1)}, f32[2,1,256,128]{3,2,1,0:T(8,128)S(1)}, u32[]{:S(2)}, u32[]{:S(2)}) collective-permute-start(f32[2,1,256,128]{3,2,1,0:T(8,128)S(1)} %get-tuple-element.414), channel_id=1, source_target_pairs={{0,16},{16,32},{32,48},{48,64},{64,80},{80,96},{96,112},{112,128},... | collective-permute-start | bytes 786440 | tf_op jit(solution)/shard_map/while/body/eval_jaxpr/ppermute | solution.py:15
  135.5 5.6 %collective-permute-start = (bf16[2,1,256,128]{3,2,1,0:T(8,128)(2,1)S(1)}, bf16[2,1,256,128]{3,2,1,0:T(8,128)(2,1)S(1)}, u32[]{:S(2)}, u32[]{:S(2)}) collective-permute-start(bf16[2,1,256,128]{3,2,1,0:T(8,128)(2,1)S(1)} %get-tuple-element.413), channel_id=1, source_target_pairs={{0,16},{16,32},{32,48},{48,64},{64,80},{80,96},{96,112},{112,128},... | collective-permute-start | bytes 393224 | tf_op jit(solution)/shard_map/while/body/eval_jaxpr/ppermute | solution.py:15
  135.5 8.4 %collective-permute-start.1 = (f32[2,1,256,128]{3,2,1,0:T(8,128)S(1)}, f32[2,1,256,128]{3,2,1,0:T(8,128)S(1)}, u32[]{:S(2)}, u32[]{:S(2)}) collective-permute-start(f32[2,1,256,128]{3,2,1,0:T(8,128)S(1)} %get-tuple-element.414), channel_id=1, source_target_pairs={{0,16},{16,32},{32,48},{48,64},{64,80},{80,96},{96,112},{112,128},... | collective-permute-start | bytes 786440 | tf_op jit(solution)/shard_map/while/body/eval_jaxpr/ppermute | solution.py:15
  144.0 5.6 %collective-permute-start = (bf16[2,1,256,128]{3,2,1,0:T(8,128)(2,1)S(1)}, bf16[2,1,256,128]{3,2,1,0:T(8,128)(2,1)S(1)}, u32[]{:S(2)}, u32[]{:S(2)}) collective-permute-start(bf16[2,1,256,128]{3,2,1,0:T(8,128)(2,1)S(1)} %get-tuple-element.413), channel_id=1, source_target_pairs={{0,16},{16,32},{32,48},{48,64},{64,80},{80,96},{96,112},{112,128},... | collective-permute-start | bytes 393224 | tf_op jit(solution)/shard_map/while/body/eval_jaxpr/ppermute | solution.py:15
  144.0 8.4 %collective-permute-start.1 = (f32[2,1,256,128]{3,2,1,0:T(8,128)S(1)}, f32[2,1,256,128]{3,2,1,0:T(8,128)S(1)}, u32[]{:S(2)}, u32[]{:S(2)}) collective-permute-start(f32[2,1,256,128]{3,2,1,0:T(8,128)S(1)} %get-tuple-element.414), channel_id=1, source_target_pairs={{0,16},{16,32},{32,48},{48,64},{64,80},{80,96},{96,112},{112,128},... | collective-permute-start | bytes 786440 | tf_op jit(solution)/shard_map/while/body/eval_jaxpr/ppermute | solution.py:15
  152.5 5.6 %collective-permute-start = (bf16[2,1,256,128]{3,2,1,0:T(8,128)(2,1)S(1)}, bf16[2,1,256,128]{3,2,1,0:T(8,128)(2,1)S(1)}, u32[]{:S(2)}, u32[]{:S(2)}) collective-permute-start(bf16[2,1,256,128]{3,2,1,0:T(8,128)(2,1)S(1)} %get-tuple-element.413), channel_id=1, source_target_pairs={{0,16},{16,32},{32,48},{48,64},{64,80},{80,96},{96,112},{112,128},... | collective-permute-start | bytes 393224 | tf_op jit(solution)/shard_map/while/body/eval_jaxpr/ppermute | solution.py:15
  152.5 8.4 %collective-permute-start.1 = (f32[2,1,256,128]{3,2,1,0:T(8,128)S(1)}, f32[2,1,256,128]{3,2,1,0:T(8,128)S(1)}, u32[]{:S(2)}, u32[]{:S(2)}) collective-permute-start(f32[2,1,256,128]{3,2,1,0:T(8,128)S(1)} %get-tuple-element.414), channel_id=1, source_target_pairs={{0,16},{16,32},{32,48},{48,64},{64,80},{80,96},{96,112},{112,128},... | collective-permute-start | bytes 786440 | tf_op jit(solution)/shard_map/while/body/eval_jaxpr/ppermute | solution.py:15
  161.0 5.6 %collective-permute-start = (bf16[2,1,256,128]{3,2,1,0:T(8,128)(2,1)S(1)}, bf16[2,1,256,128]{3,2,1,0:T(8,128)(2,1)S(1)}, u32[]{:S(2)}, u32[]{:S(2)}) collective-permute-start(bf16[2,1,256,128]{3,2,1,0:T(8,128)(2,1)S(1)} %get-tuple-element.413), channel_id=1, source_target_pairs={{0,16},{16,32},{32,48},{48,64},{64,80},{80,96},{96,112},{112,128},... | collective-permute-start | bytes 393224 | tf_op jit(solution)/shard_map/while/body/eval_jaxpr/ppermute | solution.py:15
  161.0 8.4 %collective-permute-start.1 = (f32[2,1,256,128]{3,2,1,0:T(8,128)S(1)}, f32[2,1,256,128]{3,2,1,0:T(8,128)S(1)}, u32[]{:S(2)}, u32[]{:S(2)}) collective-permute-start(f32[2,1,256,128]{3,2,1,0:T(8,128)S(1)} %get-tuple-element.414), channel_id=1, source_target_pairs={{0,16},{16,32},{32,48},{48,64},{64,80},{80,96},{96,112},{112,128},... | collective-permute-start | bytes 786440 | tf_op jit(solution)/shard_map/while/body/eval_jaxpr/ppermute | solution.py:15
  169.4 5.6 %collective-permute-start = (bf16[2,1,256,128]{3,2,1,0:T(8,128)(2,1)S(1)}, bf16[2,1,256,128]{3,2,1,0:T(8,128)(2,1)S(1)}, u32[]{:S(2)}, u32[]{:S(2)}) collective-permute-start(bf16[2,1,256,128]{3,2,1,0:T(8,128)(2,1)S(1)} %get-tuple-element.413), channel_id=1, source_target_pairs={{0,16},{16,32},{32,48},{48,64},{64,80},{80,96},{96,112},{112,128},... | collective-permute-start | bytes 393224 | tf_op jit(solution)/shard_map/while/body/eval_jaxpr/ppermute | solution.py:15
  169.5 8.4 %collective-permute-start.1 = (f32[2,1,256,128]{3,2,1,0:T(8,128)S(1)}, f32[2,1,256,128]{3,2,1,0:T(8,128)S(1)}, u32[]{:S(2)}, u32[]{:S(2)}) collective-permute-start(f32[2,1,256,128]{3,2,1,0:T(8,128)S(1)} %get-tuple-element.414), channel_id=1, source_target_pairs={{0,16},{16,32},{32,48},{48,64},{64,80},{80,96},{96,112},{112,128},... | collective-permute-start | bytes 786440 | tf_op jit(solution)/shard_map/while/body/eval_jaxpr/ppermute | solution.py:15
  177.9 5.6 %collective-permute-start = (bf16[2,1,256,128]{3,2,1,0:T(8,128)(2,1)S(1)}, bf16[2,1,256,128]{3,2,1,0:T(8,128)(2,1)S(1)}, u32[]{:S(2)}, u32[]{:S(2)}) collective-permute-start(bf16[2,1,256,128]{3,2,1,0:T(8,128)(2,1)S(1)} %get-tuple-element.413), channel_id=1, source_target_pairs={{0,16},{16,32},{32,48},{48,64},{64,80},{80,96},{96,112},{112,128},... | collective-permute-start | bytes 393224 | tf_op jit(solution)/shard_map/while/body/eval_jaxpr/ppermute | solution.py:15
  177.9 8.4 %collective-permute-start.1 = (f32[2,1,256,128]{3,2,1,0:T(8,128)S(1)}, f32[2,1,256,128]{3,2,1,0:T(8,128)S(1)}, u32[]{:S(2)}, u32[]{:S(2)}) collective-permute-start(f32[2,1,256,128]{3,2,1,0:T(8,128)S(1)} %get-tuple-element.414), channel_id=1, source_target_pairs={{0,16},{16,32},{32,48},{48,64},{64,80},{80,96},{96,112},{112,128},... | collective-permute-start | bytes 786440 | tf_op jit(solution)/shard_map/while/body/eval_jaxpr/ppermute | solution.py:15
  186.4 5.6 %collective-permute-start = (bf16[2,1,256,128]{3,2,1,0:T(8,128)(2,1)S(1)}, bf16[2,1,256,128]{3,2,1,0:T(8,128)(2,1)S(1)}, u32[]{:S(2)}, u32[]{:S(2)}) collective-permute-start(bf16[2,1,256,128]{3,2,1,0:T(8,128)(2,1)S(1)} %get-tuple-element.413), channel_id=1, source_target_pairs={{0,16},{16,32},{32,48},{48,64},{64,80},{80,96},{96,112},{112,128},... | collective-permute-start | bytes 393224 | tf_op jit(solution)/shard_map/while/body/eval_jaxpr/ppermute | solution.py:15
  186.4 8.4 %collective-permute-start.1 = (f32[2,1,256,128]{3,2,1,0:T(8,128)S(1)}, f32[2,1,256,128]{3,2,1,0:T(8,128)S(1)}, u32[]{:S(2)}, u32[]{:S(2)}) collective-permute-start(f32[2,1,256,128]{3,2,1,0:T(8,128)S(1)} %get-tuple-element.414), channel_id=1, source_target_pairs={{0,16},{16,32},{32,48},{48,64},{64,80},{80,96},{96,112},{112,128},... | collective-permute-start | bytes 786440 | tf_op jit(solution)/shard_map/while/body/eval_jaxpr/ppermute | solution.py:15
  194.9 5.6 %collective-permute-start = (bf16[2,1,256,128]{3,2,1,0:T(8,128)(2,1)S(1)}, bf16[2,1,256,128]{3,2,1,0:T(8,128)(2,1)S(1)}, u32[]{:S(2)}, u32[]{:S(2)}) collective-permute-start(bf16[2,1,256,128]{3,2,1,0:T(8,128)(2,1)S(1)} %get-tuple-element.413), channel_id=1, source_target_pairs={{0,16},{16,32},{32,48},{48,64},{64,80},{80,96},{96,112},{112,128},... | collective-permute-start | bytes 393224 | tf_op jit(solution)/shard_map/while/body/eval_jaxpr/ppermute | solution.py:15
  194.9 8.4 %collective-permute-start.1 = (f32[2,1,256,128]{3,2,1,0:T(8,128)S(1)}, f32[2,1,256,128]{3,2,1,0:T(8,128)S(1)}, u32[]{:S(2)}, u32[]{:S(2)}) collective-permute-start(f32[2,1,256,128]{3,2,1,0:T(8,128)S(1)} %get-tuple-element.414), channel_id=1, source_target_pairs={{0,16},{16,32},{32,48},{48,64},{64,80},{80,96},{96,112},{112,128},... | collective-permute-start | bytes 786440 | tf_op jit(solution)/shard_map/while/body/eval_jaxpr/ppermute | solution.py:15
  203.4 5.6 %collective-permute-start = (bf16[2,1,256,128]{3,2,1,0:T(8,128)(2,1)S(1)}, bf16[2,1,256,128]{3,2,1,0:T(8,128)(2,1)S(1)}, u32[]{:S(2)}, u32[]{:S(2)}) collective-permute-start(bf16[2,1,256,128]{3,2,1,0:T(8,128)(2,1)S(1)} %get-tuple-element.413), channel_id=1, source_target_pairs={{0,16},{16,32},{32,48},{48,64},{64,80},{80,96},{96,112},{112,128},... | collective-permute-start | bytes 393224 | tf_op jit(solution)/shard_map/while/body/eval_jaxpr/ppermute | solution.py:15
  203.4 8.4 %collective-permute-start.1 = (f32[2,1,256,128]{3,2,1,0:T(8,128)S(1)}, f32[2,1,256,128]{3,2,1,0:T(8,128)S(1)}, u32[]{:S(2)}, u32[]{:S(2)}) collective-permute-start(f32[2,1,256,128]{3,2,1,0:T(8,128)S(1)} %get-tuple-element.414), channel_id=1, source_target_pairs={{0,16},{16,32},{32,48},{48,64},{64,80},{80,96},{96,112},{112,128},... | collective-permute-start | bytes 786440 | tf_op jit(solution)/shard_map/while/body/eval_jaxpr/ppermute | solution.py:15
  211.8 5.6 %collective-permute-start = (bf16[2,1,256,128]{3,2,1,0:T(8,128)(2,1)S(1)}, bf16[2,1,256,128]{3,2,1,0:T(8,128)(2,1)S(1)}, u32[]{:S(2)}, u32[]{:S(2)}) collective-permute-start(bf16[2,1,256,128]{3,2,1,0:T(8,128)(2,1)S(1)} %get-tuple-element.413), channel_id=1, source_target_pairs={{0,16},{16,32},{32,48},{48,64},{64,80},{80,96},{96,112},{112,128},... | collective-permute-start | bytes 393224 | tf_op jit(solution)/shard_map/while/body/eval_jaxpr/ppermute | solution.py:15
  211.9 8.4 %collective-permute-start.1 = (f32[2,1,256,128]{3,2,1,0:T(8,128)S(1)}, f32[2,1,256,128]{3,2,1,0:T(8,128)S(1)}, u32[]{:S(2)}, u32[]{:S(2)}) collective-permute-start(f32[2,1,256,128]{3,2,1,0:T(8,128)S(1)} %get-tuple-element.414), channel_id=1, source_target_pairs={{0,16},{16,32},{32,48},{48,64},{64,80},{80,96},{96,112},{112,128},... | collective-permute-start | bytes 786440 | tf_op jit(solution)/shard_map/while/body/eval_jaxpr/ppermute | solution.py:15
  220.3 7.2 %collective-permute-start.2 = (f32[2,1,256,128]{3,2,0,1:T(8,128)S(1)}, f32[2,1,256,128]{3,2,0,1:T(8,128)S(1)}, u32[]{:S(2)}, u32[]{:S(2)}) collective-permute-start(f32[2,1,256,128]{3,2,0,1:T(8,128)S(1)} %bitcast.163), channel_id=1, source_target_pairs={{0,16},{16,32},{32,48},{48,64},{64,80},{80,96},{96,112},{112,128},... | collective-permute-start | bytes 786440 | tf_op jit(solution)/shard_map/ppermute | solution.py:15
  221.1 11.2 %all-to-all-start = ((bf16[128,1,4,128]{3,2,1,0:T(4,128)(2,1)}), bf16[128,1,4,128]{3,2,1,0:T(4,128)(2,1)S(1)}, u32[]{:S(2)}, u32[]{:S(2)}) async-start(bf16[128,1,4,128]{3,2,1,0:T(4,128)(2,1)} %bitcast.19), calls=%async_computation | async-start | bytes 262144 | tf_op jit(solution)/shard_map/all_to_all | solution.py:155
  232.2 18.2 %all-to-all-start.3 = ((bf16[128,1,8,128]{3,2,1,0:T(8,128)(2,1)}), bf16[128,1,8,128]{3,2,1,0:T(8,128)(2,1)S(1)}, u32[]{:S(2)}, u32[]{:S(2)}) async-start(bf16[128,1,8,128]{3,2,1,0:T(8,128)(2,1)} %slice_bitcast_fusion.9), calls=%async_computation.3 | async-start | bytes 524288 | tf_op jit(solution)/shard_map/all_to_all | solution.py:158
  250.4 10.6 %all-to-all-start.1 = ((bf16[8,2,1024]{2,1,0:T(2,128)(2,1)}), bf16[8,2,1024]{2,1,0:T(2,128)(2,1)S(1)}, u32[]{:S(2)}, u32[]{:S(2)}) async-start(bf16[8,2,1024]{2,1,0:T(2,128)(2,1)} %reshape.660), calls=%async_computation.1 | async-start | bytes 65536 | tf_op jit(solution)/shard_map/all_to_all | solution.py:156
  261.1 9.5 %all-to-all-start.2 = ((bf16[8,2,1024]{2,1,0:T(2,128)(2,1)}), bf16[8,2,1024]{2,1,0:T(2,128)(2,1)S(1)}, u32[]{:S(2)}, u32[]{:S(2)}) async-start(bf16[8,2,1024]{2,1,0:T(2,128)(2,1)} %reshape.662), calls=%async_computation.2 | async-start | bytes 65536 | tf_op jit(solution)/shard_map/all_to_all | solution.py:157
  270.6 9.5 %all-to-all-start.4 = ((bf16[8,2,1024]{2,1,0:T(2,128)(2,1)}), bf16[8,2,1024]{2,1,0:T(2,128)(2,1)S(1)}, u32[]{:S(2)}, u32[]{:S(2)}) async-start(bf16[8,2,1024]{2,1,0:T(2,128)(2,1)} %reshape.664), calls=%async_computation.4 | async-start | bytes 65536 | tf_op jit(solution)/shard_map/all_to_all | solution.py:159
  280.1 9.5 %all-to-all-start.5 = ((bf16[8,2,1024]{2,1,0:T(2,128)(2,1)}), bf16[8,2,1024]{2,1,0:T(2,128)(2,1)S(1)}, u32[]{:S(2)}, u32[]{:S(2)}) async-start(bf16[8,2,1024]{2,1,0:T(2,128)(2,1)} %reshape.666), calls=%async_computation.5 | async-start | bytes 65536 | tf_op jit(solution)/shard_map/all_to_all | solution.py:160
Sparse Core Ops, SparseCore 0:
  10.5 42.6 all-gather.2
where the time goes:
time: 298 us; the launch traced here: 297 us
  waiting for transfers between devices  125 us (42%)
  matrix products  59.3 us (20%)
  starting transfers between devices  31.4 us (11%)
  other arithmetic  25 us (8%)
  local copies, waits for them, and re-layouts  18.6 us (6%)
  between operations  14.5 us (5%)
  blocking collectives  11.8 us (4%)
  loops' own time  11.3 us (4%)
    ppermute x31, waiting for transfers between devices, shifted(): return lax.ppermute(value, axis, pairs)  70.4 us
    all_gather x1, waiting for transfers between devices, on_device(): lax.all_gather(key_value, 'blk', axis=2, tiled=True)  38.1 us
    dot_general x17, matrix products, scores_of(): jnp.einsum('gqd,gkd->gqk', queries, pieces[0], preferred_element_type=jnp...  20.8 us
    dot_general x17, matrix products, scores_of(): jnp.einsum('gqd,gkd->gqk', grad_outs, pieces[1], preferred_element_type=j...  19.3 us
    reduce_sum x1, other arithmetic, on_device(): running_sum = jnp.sum(weights, axis=2)  11.9 us
    psum x1, blocking collectives, on_device(): summed = lax.psum(pref_grads, 'pair').astype(jnp.bfloat16)  11.8 us
    another operation x1, loops' own time, on_device(): lax.scan(back_turn, (key_value, grads_held, dq_sum), jnp.arange(1, cycle_...  11.3 us
    dynamic_slice x15, local copies, waits for them, and re-layouts, on_device(): lax.scan(back_turn, (key_value, grads_held, dq_sum), jnp.arange(1, cycle_...  8.83 us
  transfers between devices with their start and end apart: 38, of which 36 were waited for; matrix products, arithmetic and copies ran while one was open for 20% of the time, Pallas kernels for 0%

commit v1 on v0

v1 whole, which is shorter than its diff:
```python
import functools

import jax
import jax.numpy as jnp
from jax import lax
from jax.experimental import pallas as pl
from jax.experimental.pallas import tpu as pltpu
from jax.sharding import PartitionSpec as P

MESH = pl.DeviceIdType.MESH
F32 = jnp.float32
BF = jnp.bfloat16
I32 = jnp.int32
LANES = 128
SCALE = LANES ** -0.5
C = SCALE * 1.4426950408889634
LOW = -1e30
TW = 512
GW = 256
NP = 512
NR = 1024
NQ = NP + NR


def dot(a, b):
    return lax.dot_general(a, b, (((1,), (0,)), ((), ())), preferred_element_type=F32)


def masked(s, diff, t0, t1, fill):
    n = s.shape[0] // 2
    return jnp.concatenate(
        [jnp.where(diff <= t0, s[:n], fill), jnp.where(diff <= t1, s[n:], fill)], axis=0
    )


def kernel(
    order, lengths, pq, pdo, rq, rdo, pk, pv, rk, rv,
    o_dqp, o_dqr, o_pkv, o_rkv,
    kv, q, do, q_t, do_t, m, l, d, lse, dl, dq_t, diff_p, diff_r,
    s_pre, dp_pre, s_res, dp_res,
    acc, sib_out, sib_in, ring_out, l_in, r_in, fin, dq,
    in_sem, ag_recv, ag_ring_send, ag_sib_send,
    rs_sib_send, rs_sib_recv, rs_send, l_recv, r_recv,
    dq_send, dq_recv, kv_send, kv_recv, px_send, px_recv, loc_sem,
):
    b = lax.axis_index("blk")
    pair = lax.axis_index("pair")
    head = lax.axis_index("head")
    z = b // 2
    c = b % 2
    sib = b + 1 - 2 * c
    right = lax.rem(b + 2, 16)
    left = lax.rem(b + 14, 16)

    barrier = pltpu.get_barrier_semaphore()
    for n in (sib, right, left):
        pl.semaphore_signal(barrier, inc=1, device_id={"blk": n}, device_id_type=MESH)
    for k in range(1, 8):
        pl.semaphore_signal(
            barrier, inc=1, device_id={"head": lax.rem(head + k, 8)}, device_id_type=MESH
        )
    for k in range(8):
        pl.semaphore_signal(
            barrier, inc=1, device_id={"pair": 1 - pair, "head": lax.rem(head + k, 8)},
            device_id_type=MESH,
        )

    def rows_of(block):
        return pl.ds(pl.multiple_of(block * 128, 128), 128)

    loads = [
        pltpu.make_async_copy(ref, kv.at[i, rows_of(b), :], in_sem.at[i])
        for i, ref in enumerate((pk, pv, rk, rv))
    ] + [
        pltpu.make_async_copy(ref, dst, in_sem.at[4 + i])
        for i, (ref, dst) in enumerate((
            (pq, q.at[pl.ds(0, NP), :]),
            (rq, q.at[pl.ds(NP, NR), :]),
            (pdo, do.at[pl.ds(0, NP), :]),
            (rdo, do.at[pl.ds(NP, NR), :]),
        ))
    ]
    for copy in loads:
        copy.start()

    def kv_copy(h, block, send_sem, target):
        piece = kv.at[pl.ds(2 * h, 2), rows_of(block), :]
        return pltpu.make_async_remote_copy(
            src_ref=piece, dst_ref=piece, send_sem=send_sem, recv_sem=ag_recv.at[h, block],
            device_id={"blk": target}, device_id_type=MESH,
        )

    for copy in loads[:4]:
        copy.wait()
    pl.semaphore_wait(barrier, 18)
    for h in range(2):
        kv_copy(h, b, ag_ring_send.at[h, 0], right).start()
        kv_copy(h, b, ag_ring_send.at[h, 4], left).start()
        kv_copy(h, b, ag_sib_send.at[h, 0], sib).start()

    for copy in loads[4:]:
        copy.wait()
    live = b * 128 < lengths[pair]
    do[NP:, :] = jnp.where(live, do[NP:, :].astype(F32), 0.0).astype(BF)
    q_t[...] = q[...].T
    do_t[...] = do[...].T
    m[...] = jnp.full(m.shape, LOW, F32)
    l[...] = jnp.zeros(l.shape, F32)
    d[...] = jnp.zeros(d.shape, F32)
    dq_t[...] = jnp.zeros(dq_t.shape, F32)
    key_row = lax.broadcasted_iota(I32, (128, TW), 0)
    column = lax.broadcasted_iota(I32, (128, TW), 1)
    diff_p[...] = key_row - column // 4
    diff_r[...] = key_row - column // 8

    def thresholds(zp, h, tile):
        if h == 0:
            if tile > 0:
                return ()
            own = order[b]
            return (diff_p[...], (own - order[2 * zp]) * 128, (own - order[2 * zp + 1]) * 128)
        t0 = (b - 2 * zp) * 128 + (tile - 1) * (TW // 8)
        return (diff_r[...], t0, t0 - 128)

    def keys_of(zp, h):
        rows = pl.ds(pl.multiple_of(zp * 256, 256), 256)
        return kv[2 * h, rows, :], kv[2 * h + 1, rows, :]

    stored = ((s_pre, dp_pre), (s_res, dp_res))

    def totals_unit(zp, h):
        k, v = keys_of(zp, h)
        rows = pl.ds(pl.multiple_of(zp * 256, 256), 256)
        for tile in range(h, NQ // TW):
            cs = pl.ds(tile * TW, TW)
            s = dot(k, q_t[:, cs]) * C
            dp = dot(v, do_t[:, cs])
            limits = thresholds(zp, h, tile)
            if limits:
                s = masked(s, *limits, LOW)
            there = pl.ds((tile - h) * TW, TW)
            stored[h][0][rows, there] = s
            stored[h][1][rows, there] = dp
            s = s.reshape(-1, 8, TW)
            dp = dp.reshape(-1, 8, TW)
            old = m[:, cs]
            new = jnp.maximum(old, jnp.max(s, axis=0))
            e = jnp.exp2(s - new[None])
            shrink = jnp.exp2(old - new)
            m[:, cs] = new
            l[:, cs] = l[:, cs] * shrink + jnp.sum(e, axis=0)
            d[:, cs] = d[:, cs] * shrink + jnp.sum(e * dp, axis=0)

    def take_ring(t):
        k = (t + 1) // 2
        for h in range(2):
            @pl.when(t % 2 == 1)
            def _():
                block = lax.rem(b + 16 - 2 * k, 16)
                kv_copy(h, block, ag_ring_send.at[h, 0], right).wait_recv()

                @pl.when(k < 4)
                def _():
                    kv_copy(h, block, ag_ring_send.at[h, k], right).start()

                kv_copy(h, block, ag_sib_send.at[h, t], sib).start()

            @pl.when(t % 2 == 0)
            def _():
                block = lax.rem(b + 2 * k, 16)
                kv_copy(h, block, ag_ring_send.at[h, 0], left).wait_recv()

                @pl.when(k < 3)
                def _():
                    kv_copy(h, block, ag_ring_send.at[h, 4 + k], left).start()

                kv_copy(h, block, ag_sib_send.at[h, t], sib).start()

    def totals_step(t, carry):
        @pl.when(t < 7)
        def _():
            take_ring(t + 1)

        k = (t + 1) // 2
        zp = lax.rem(jnp.where(t % 2 == 1, z + 8 - k, z + k), 8)
        for h in range(2):
            kv_copy(h, 2 * zp + 1 - c, ag_sib_send.at[h, 0], sib).wait_recv()
        totals_unit(zp, 0)

        @pl.when(zp <= z)
        def _():
            totals_unit(zp, 1)

        return carry

    lax.fori_loop(0, 8, totals_step, 0)

    top = jnp.max(m[...], axis=0, keepdims=True)
    weight = jnp.exp2(m[...] - top)
    total = jnp.sum(l[...] * weight, axis=0, keepdims=True)
    lse[...] = top + jnp.log2(total)
    dl[...] = jnp.sum(d[...] * weight, axis=0, keepdims=True) / total

    def grads_unit(zp, h):
        rows = pl.ds(pl.multiple_of(zp * 256, 256), 256)
        k_t = kv[2 * h, rows, :].T
        dk = jnp.zeros((256, LANES), F32)
        dv = jnp.zeros((256, LANES), F32)
        for tile in range((NQ - h * NP) // GW):
            there = pl.ds(tile * GW, GW)
            cs = pl.ds(h * NP + tile * GW, GW)
            p = jnp.exp2(stored[h][0][rows, there] - lse[:, cs])
            ds = (p * (stored[h][1][rows, there] - dl[:, cs]) * SCALE).astype(BF)
            dk += dot(ds, q[cs, :])
            dv += dot(p.astype(BF), do[cs, :])
            dq_t[:, cs] += dot(k_t, ds)
        for i, part in ((0, dk), (1, dv)):
            acc[h, 0, i] = part[:128]
            acc[h, 1, i] = part[128:]

    def sib_copy(t, h):
        return pltpu.make_async_remote_copy(
            src_ref=sib_out.at[t, h], dst_ref=sib_in.at[t, h], send_sem=rs_sib_send.at[t, h],
            recv_sem=rs_sib_recv.at[t, h], device_id={"blk": sib}, device_id_type=MESH,
        )

    def left_copy(dist, h):
        return pltpu.make_async_remote_copy(
            src_ref=ring_out.at[dist - 1, h], dst_ref=l_in.at[dist - 1, h],
            send_sem=rs_send.at[dist - 1, h], recv_sem=l_recv.at[dist - 1, h],
            device_id={"blk": left}, device_id_type=MESH,
        )

    def right_copy(dist, h):
        return pltpu.make_async_remote_copy(
            src_ref=ring_out.at[dist + 3, h], dst_ref=r_in.at[dist - 1, h],
            send_sem=rs_send.at[dist + 3, h], recv_sem=r_recv.at[dist - 1, h],
            device_id={"blk": right}, device_id_type=MESH,
        )

    def compute(t, h):
        half = (t + 1) // 2
        zp = lax.rem(jnp.where(t % 2 == 0, z + 4 + half, z + 12 - half), 8)
        if h == 0:
            grads_unit(zp, 0)
        else:
            @pl.when(zp <= z)
            def _():
                grads_unit(zp, 1)

            @pl.when(zp > z)
            def _():
                acc[1] = jnp.zeros(acc.shape[1:], F32)

        sib_out[t, h] = acc[h, 1 - c].astype(BF)
        sib_copy(t, h).start()

    def own_and_sibling(t, h):
        sib_copy(t, h).wait_recv()
        return acc[h, c] + sib_in[t, h].astype(F32)

    def finalize(t, h):
        half = (t + 1) // 2
        dist = 4 - half
        part = own_and_sibling(t, h)

        @pl.when(t % 2 == 0)
        def _():
            @pl.when(dist == 4)
            def _():
                ring_out[dist - 1, h] = part.astype(BF)

            @pl.when(dist < 4)
            def _():
                left_copy(dist + 1, h).wait_recv()
                ring_out[dist - 1, h] = (part + l_in[dist, h].astype(F32)).astype(BF)

            left_copy(dist, h).start()

        @pl.when(t % 2 == 1)
        def _():
            @pl.when(dist == 3)
            def _():
                ring_out[dist + 3, h] = part.astype(BF)

            @pl.when(dist < 3)
            def _():
                right_copy(dist + 1, h).wait_recv()
                ring_out[dist + 3, h] = (part + r_in[dist, h].astype(F32)).astype(BF)

            right_copy(dist, h).start()

    def grads_step(t, carry):
        compute(t, 0)

        @pl.when(t > 0)
        def _():
            finalize(t - 1, 1)

        compute(t, 1)

        @pl.when(t < 7)
        def _():
            finalize(t, 0)

        return carry

    lax.fori_loop(0, 8, grads_step, 0)

    def peer(k, other):
        where = {"head": lax.rem(head + k, 8)}
        if other:
            where["pair"] = 1 - pair
        return where

    def to_heads(k, src, dst, send_sem, recv_sem, other=False):
        return pltpu.make_async_remote_copy(
            src_ref=src, dst_ref=dst, send_sem=send_sem, recv_sem=recv_sem,
            device_id=peer(k, other), device_id_type=MESH,
        )

    def dq_copies(k):
        h = lax.rem(head + k, 8)
        rows_p = dq.at[pl.ds(pl.multiple_of(h * 64, 64), 64), :]
        rows_r = dq.at[pl.ds(pl.multiple_of(NP + h * 128, 128), 128), :]
        return ((rows_p, o_dqp.at[head]), (rows_r, o_dqr.at[head]))

    def kv_pieces(k):
        h = lax.rem(head + k, 8)
        rows = pl.ds(pl.multiple_of(h * 16, 16), 16)
        return (fin.at[0, :, rows, :], o_pkv.at[pair, :, head]), (
            fin.at[1, :, rows, :], o_rkv.at[:, head])

    dq[...] = dq_t[...].T.astype(BF)
    pending = []
    local = []
    for k in range(1, 8):
        for i, (src, dst) in enumerate(dq_copies(k)):
            copy = to_heads(k, src, dst, dq_send.at[i, k], dq_recv.at[i, k])
            copy.start()
            pending.append(copy)
    for i, (src, dst) in enumerate(dq_copies(0)):
        copy = pltpu.make_async_copy(src, dst, loc_sem.at[i])
        copy.start()
        local.append(copy)

    for h in range(2):
        part = own_and_sibling(7, h)
        left_copy(1, h).wait_recv()
        right_copy(1, h).wait_recv()
        fin[h] = (part + l_in[0, h].astype(F32) + r_in[0, h].astype(F32)).astype(BF)
    for k in range(0, 8):
        src, dst = kv_pieces(k)[0]
        copy = to_heads(k, src, dst, px_send.at[k], px_recv.at[k], other=True)
        copy.start()
        pending.append(copy)
    for k in range(1, 8):
        for i, (src, dst) in enumerate(kv_pieces(k)):
            copy = to_heads(k, src, dst, kv_send.at[i, k], kv_recv.at[i, k])
            copy.start()
            pending.append(copy)
    for i, (src, dst) in enumerate(kv_pieces(0)):
        copy = pltpu.make_async_copy(src, dst, loc_sem.at[2 + i])
        copy.start()
        local.append(copy)

    for h in range(2):
        for k in range(7):
            kv_copy(h, b, ag_ring_send.at[h, k], right).wait_send()
        for k in range(8):
            kv_copy(h, b, ag_sib_send.at[h, k], sib).wait_send()
        for t in range(8):
            sib_copy(t, h).wait_send()
        for dist in range(1, 5):
            left_copy(dist, h).wait_send()
        for dist in range(1, 4):
            right_copy(dist, h).wait_send()
    for copy in local:
        copy.wait()
    for copy in pending:
        copy.wait()


def place(dqp, dqr, pkv, rkv, o_pq, o_pk, o_pv, o_rq, o_rk, o_rv, b_pq, b_rq, b_kv, sems):
    copies = []

    def send(i, src, dst):
        copy = pltpu.make_async_copy(src, dst, sems.at[i])
        copy.start()
        copies.append(copy)

    for g in range(8):
        b_rq[:, g] = dqr[g]
    send(0, b_rq, o_rq)
    for g in range(8):
        b_pq[:, g] = dqp[g]
    send(1, b_pq, o_pq)
    to = lax.broadcasted_iota(I32, (128, 128), 0)
    source = lax.broadcasted_iota(I32, (128, 128), 1)
    move = jnp.where(source == (to % 8) * 16 + to // 8, 1.0, 0.0).astype(BF)
    for i, out in enumerate((o_pk, o_pv, o_rk, o_rv)):
        if i < 2:
            rows = dot(move, pkv[0, i]) + dot(move, pkv[1, i])
        else:
            rows = dot(move, rkv[i - 2])
        b_kv[i] = rows.astype(BF)
        send(2 + i, b_kv.at[i], out)
    for copy in copies:
        copy.wait()


def on_device(
    prefix_query_rows,
    prefix_key_rows,
    prefix_value_rows,
    prefix_output_gradient,
    resp_q,
    resp_k,
    response_value_rows,
    response_output_gradient,
    lengths,
    prefix_order,
):
    vm = pltpu.VMEM
    dma = pltpu.SemaphoreType.DMA
    out = jax.ShapeDtypeStruct
    dqp, dqr, pkv, rkv = pl.pallas_call(
        kernel,
        out_shape=(
            out((8, 64, LANES), BF),
            out((8, 128, LANES), BF),
            out((2, 2, 8, 16, LANES), BF),
            out((2, 8, 16, LANES), BF),
        ),
        in_specs=[pl.BlockSpec(memory_space=pltpu.SMEM)] * 2
        + [pl.BlockSpec(memory_space=pltpu.HBM)] * 8,
        out_specs=[pl.BlockSpec(memory_space=pl.ANY)] * 4,
        scratch_shapes=[
            vm((4, 2048, LANES), BF),
            vm((NQ, LANES), BF),
            vm((NQ, LANES), BF),
            vm((LANES, NQ), BF),
            vm((LANES, NQ), BF),
            vm((8, NQ), F32),
            vm((8, NQ), F32),
            vm((8, NQ), F32),
            vm((1, NQ), F32),
            vm((1, NQ), F32),
            vm((LANES, NQ), F32),
            vm((128, TW), I32),
            vm((128, TW), I32),
            vm((2048, NQ), F32),
            vm((2048, NQ), F32),
            vm((2048, NR), F32),
            vm((2048, NR), F32),
            vm((2, 2, 2, 128, LANES), F32),
            vm((8, 2, 2, 128, LANES), BF),
            vm((8, 2, 2, 128, LANES), BF),
            vm((7, 2, 2, 128, LANES), BF),
            vm((4, 2, 2, 128, LANES), BF),
            vm((3, 2, 2, 128, LANES), BF),
            vm((2, 2, 128, LANES), BF),
            vm((NQ, LANES), BF),
            dma((8,)),
            dma((2, 16)),
            dma((2, 7)),
            dma((2, 8)),
            dma((8, 2)),
            dma((8, 2)),
            dma((7, 2)),
            dma((4, 2)),
            dma((3, 2)),
            dma((2, 8)),
            dma((2, 8)),
            dma((2, 8)),
            dma((2, 8)),
            dma((8,)),
            dma((8,)),
            dma((4,)),
        ],
        compiler_params=pltpu.CompilerParams(
            collective_id=0, has_side_effects=True, vmem_limit_bytes=56 << 20
        ),
    )(
        prefix_order,
        lengths,
        prefix_query_rows.reshape(NP, LANES),
        prefix_output_gradient.reshape(NP, LANES),
        resp_q.reshape(NR, LANES),
        response_output_gradient.reshape(NR, LANES),
        prefix_key_rows.reshape(128, LANES),
        prefix_value_rows.reshape(128, LANES),
        resp_k.reshape(128, LANES),
        response_value_rows.reshape(128, LANES),
    )
    any_space = pl.BlockSpec(memory_space=pl.ANY)
    vmem_space = pl.BlockSpec(memory_space=pltpu.VMEM)
    return pl.pallas_call(
        place,
        out_shape=(
            out((16, 8, 4, LANES), BF),
            out((128, LANES), BF),
            out((128, LANES), BF),
            out((16, 8, 8, LANES), BF),
            out((128, LANES), BF),
            out((128, LANES), BF),
        ),
        in_specs=[vmem_space] * 4,
        out_specs=[any_space] * 6,
        scratch_shapes=[
            vm((16, 8, 4, LANES), BF),
            vm((16, 8, 8, LANES), BF),
            vm((4, 128, LANES), BF),
            dma((6,)),
        ],
    )(
        dqp.reshape(8, 16, 4, LANES),
        dqr.reshape(8, 16, 8, LANES),
        pkv.reshape(2, 2, 128, LANES),
        rkv.reshape(2, 128, LANES),
    )


def shaped(*args):
    pq, pk, pv, rq, rk, rv = on_device(*args)
    keys = (16, 8, LANES)
    return (
        pq, pk.reshape(keys), pv.reshape(keys),
        rq[None], rk.reshape(keys)[None], rv.reshape(keys)[None],
    )


def solution(mesh):
    in_specs = (
        P("blk", "head", "pair", None),
        P("blk", "head", None),
        P("blk", "head", None),
        P("blk", "head", "pair", None),
        P("pair", "blk", "head", None, None),
        P("pair", "blk", "head", None),
        P("pair", "blk", "head", None),
        P("pair", "blk", "head", None, None),
        P(),
        P(),
    )
    out_specs = (
        P(("blk", "head"), None, "pair", None),
        P(("blk", "head"), None, None),
        P(("blk", "head"), None, None),
        P("pair", ("blk", "head"), None, None, None),
        P("pair", ("blk", "head"), None, None),
        P("pair", ("blk", "head"), None, None),
    )
    return jax.shard_map(
        shaped, mesh=mesh, in_specs=in_specs, out_specs=out_specs, check_vma=False
    )
```

time: 298 us -> 59.9 us (0.20)
  the two profiles are of different devices: /device:TPU:2 before, /device:TPU:1 now
where the time goes in v1:
time: 59.9 us; the launch traced here: 59.7 us
  Pallas kernels  59.1 us (99%)
  between operations  0.64 us (1%)
    pallas_call x1, Pallas kernels, on_device(): pl.pallas_call(kernel, out_shape=(out((8, 64, LANES), BF), out((8, 128, L...  57.1 us
    pallas_call x1, Pallas kernels, on_device(): pl.pallas_call(place, out_shape=(out((16, 8, 4, LANES), BF), out((128, LA...  1.97 us

profile of v1, /device:TPU:1, one launch (start us, length us, event | category | flops | bytes accessed | tf_op | source)
XLA Modules:
  0.0 59.7 jit_solution(11027137511556807524)
XLA Ops:
  0.6 57.1 %shard_map.145 = (bf16[8,64,128]{2,1,0:T(8,128)(2,1)}, bf16[8,128,128]{2,1,0:T(8,128)(2,1)}, bf16[2,2,8,16,128]{4,3,2,1,0:T(8,128)(2,1)}, bf16[2,8,16,128]{3,2,1,0:T(8,128)(2,1)}) custom-call(s32[16]{0:T(128)} %order.1, s32[2]{0:T(128)} %lengths.1, bf16[512,128]{1,0:T(8,128)(2,1)} %bitcast.20, bf16[512,128]{1,0:T(8,128)(2,1)} %bitcast.21, ...), custom_call_target="tpu_custom_call" | custom-call | tf_op jit(solution)/shard_map/pallas_call | solution.py:427
  57.8 2.0 %shard_map.146 = (bf16[16,8,4,128]{3,2,1,0:T(4,128)(2,1)}, bf16[128,128]{1,0:T(8,128)(2,1)}, bf16[128,128]{1,0:T(8,128)(2,1)}, bf16[16,8,8,128]{3,2,1,0:T(8,128)...) custom-call(bf16[8,16,4,128]{3,2,1,0:T(4,128)(2,1)} %bitcast.22, bf16[8,16,8,128]{3,2,1,0:T(8,128)(2,1)} %bitcast.17, ...), custom_call_target="tpu_custom_call" | custom-call | tf_op jit(solution)/shard_map/pallas_call | solution.py:498

commit v2 on v1

v2 whole, which is shorter than its diff:
```python
import functools

import jax
import jax.numpy as jnp
from jax import lax
from jax.experimental import pallas as pl
from jax.experimental.pallas import tpu as pltpu
from jax.sharding import PartitionSpec as P

MESH = pl.DeviceIdType.MESH
F32 = jnp.float32
BF = jnp.bfloat16
I32 = jnp.int32
LANES = 128
SCALE = LANES ** -0.5
C = SCALE * 1.4426950408889634
LOW = -1e30
TW = 512
GW = 256
NP = 512
NR = 1024
NQ = NP + NR


def dot(a, b):
    return lax.dot_general(a, b, (((1,), (0,)), ((), ())), preferred_element_type=F32)


def masked(s, diff, t0, t1, fill):
    n = s.shape[0] // 2
    return jnp.concatenate(
        [jnp.where(diff <= t0, s[:n], fill), jnp.where(diff <= t1, s[n:], fill)], axis=0
    )


def kernel(
    order_in, lengths_in, pq, pdo, rq, rdo, pk, pv, rk, rv,
    o_dqp, o_dqr, o_own, o_other,
    order, lengths,
    kv, q, do, q_t, do_t, m, l, d, lse, dl, dq_t, diff_p, diff_r,
    s_pre, dp_pre, s_res, dp_res,
    acc, sib_out, sib_in, ring_out, l_in, r_in, far_in, fin, dq,
    in_sem, ag_recv, ag_ring_send, ag_sib_send,
    rs_sib_send, rs_sib_recv, rs_send, l_recv, r_recv, far_recv,
    end_send, end_recv, loc_sem,
):
    b = lax.axis_index("blk")
    pair = lax.axis_index("pair")
    head = lax.axis_index("head")
    z = b // 2
    c = b % 2
    sib = b + 1 - 2 * c
    right = lax.rem(b + 2, 16)
    left = lax.rem(b + 14, 16)
    right2 = lax.rem(b + 4, 16)
    left2 = lax.rem(b + 12, 16)

    def rows_of(block):
        return pl.ds(pl.multiple_of(block * 128, 128), 128)

    loads = [
        pltpu.make_async_copy(ref, kv.at[i, rows_of(b), :], in_sem.at[i])
        for i, ref in enumerate((pk, pv, rk, rv))
    ] + [
        pltpu.make_async_copy(ref, dst, in_sem.at[4 + i])
        for i, (ref, dst) in enumerate((
            (pq, q.at[pl.ds(0, NP), :]),
            (rq, q.at[pl.ds(NP, NR), :]),
            (pdo, do.at[pl.ds(0, NP), :]),
            (rdo, do.at[pl.ds(NP, NR), :]),
            (order_in, order),
            (lengths_in, lengths),
        ))
    ]
    barrier = pltpu.get_barrier_semaphore()
    for n in (sib, right, left, right2, left2):
        pl.semaphore_signal(barrier, inc=1, device_id={"blk": n}, device_id_type=MESH)
    for k in range(1, 8):
        pl.semaphore_signal(
            barrier, inc=1, device_id={"head": lax.rem(head + k, 8)}, device_id_type=MESH
        )
    for k in range(8):
        pl.semaphore_signal(
            barrier, inc=1, device_id={"pair": 1 - pair, "head": lax.rem(head + k, 8)},
            device_id_type=MESH,
        )

    for copy in loads:
        copy.start()

    def kv_copy(i, block, send_sem, target):
        piece = kv.at[i, rows_of(block), :]
        return pltpu.make_async_remote_copy(
            src_ref=piece, dst_ref=piece, send_sem=send_sem, recv_sem=ag_recv.at[i, block],
            device_id={"blk": target}, device_id_type=MESH,
        )

    for copy in loads[:4]:
        copy.wait()
    pl.semaphore_wait(barrier, 20)
    for i in range(4):
        kv_copy(i, b, ag_ring_send, right).start()
        kv_copy(i, b, ag_ring_send, left).start()
        kv_copy(i, b, ag_sib_send, sib).start()

    for copy in loads[4:]:
        copy.wait()
    live = b * 128 < lengths[pair]
    do[NP:, :] = jnp.where(live, do[NP:, :].astype(F32), 0.0).astype(BF)
    q_t[...] = q[...].T
    do_t[...] = do[...].T
    m[...] = jnp.full(m.shape, LOW, F32)
    l[...] = jnp.zeros(l.shape, F32)
    d[...] = jnp.zeros(d.shape, F32)
    dq_t[...] = jnp.zeros(dq_t.shape, F32)
    key_row = lax.broadcasted_iota(I32, (128, TW), 0)
    column = lax.broadcasted_iota(I32, (128, TW), 1)
    diff_p[...] = key_row - column // 4
    diff_r[...] = key_row - column // 8

    def thresholds(zp, h, tile):
        if h == 0:
            if tile > 0:
                return ()
            own = order[b]
            return (diff_p[...], (own - order[2 * zp]) * 128, (own - order[2 * zp + 1]) * 128)
        t0 = (b - 2 * zp) * 128 + (tile - 1) * (TW // 8)
        return (diff_r[...], t0, t0 - 128)

    def keys_of(zp, h):
        rows = pl.ds(pl.multiple_of(zp * 256, 256), 256)
        return kv[2 * h, rows, :], kv[2 * h + 1, rows, :]

    stored = ((s_pre, dp_pre), (s_res, dp_res))

    def totals_unit(zp, h):
        k, v = keys_of(zp, h)
        rows = pl.ds(pl.multiple_of(zp * 256, 256), 256)
        for tile in range(h, NQ // TW):
            cs = pl.ds(tile * TW, TW)
            s = dot(k, q_t[:, cs]) * C
            dp = dot(v, do_t[:, cs])
            limits = thresholds(zp, h, tile)
            if limits:
                s = masked(s, *limits, LOW)
            there = pl.ds((tile - h) * TW, TW)
            stored[h][0][rows, there] = s
            stored[h][1][rows, there] = dp
            s = s.reshape(-1, 8, TW)
            dp = dp.reshape(-1, 8, TW)
            old = m[:, cs]
            new = jnp.maximum(old, jnp.max(s, axis=0))
            e = jnp.exp2(s - new[None])
            shrink = jnp.exp2(old - new)
            m[:, cs] = new
            l[:, cs] = l[:, cs] * shrink + jnp.sum(e, axis=0)
            d[:, cs] = d[:, cs] * shrink + jnp.sum(e * dp, axis=0)

    def take_ring(k):
        from_left = lax.rem(b + 16 - 2 * k, 16)
        from_right = lax.rem(b + 2 * k, 16)

        def take(i, block, target, go_on):
            kv_copy(i, block, ag_ring_send, target).wait_recv()

            @pl.when(go_on)
            def _():
                kv_copy(i, block, ag_ring_send, target).start()

            kv_copy(i, block, ag_sib_send, sib).start()

        for i in range(4):
            there = i < 2

            @pl.when((k < 4) | there)
            def _():
                take(i, from_left, right, (k < 3) | ((k == 3) & there))

            @pl.when((k < 4) | (not there))
            def _():
                take(i, from_right, left, (k < 3) | ((k == 3) & (not there)))

    def totals_step(n, carry):
        @pl.when((n == 0) | (n == 1) | (n == 3) | (n == 7))
        def _():
            take_ring(jnp.where(n == 0, 1, jnp.where(n == 7, 4, (n + 3) // 2)))

        k = (n + 1) // 2
        zp = lax.rem(jnp.where(n % 2 == 1, z + 8 - k, z + k), 8)
        for i in range(4):
            kv_copy(i, 2 * zp + 1 - c, ag_sib_send, sib).wait_recv()
        totals_unit(zp, 0)

        @pl.when(zp <= z)
        def _():
            totals_unit(zp, 1)

        return carry

    lax.fori_loop(0, 8, totals_step, 0)

    top = jnp.max(m[...], axis=0, keepdims=True)
    weight = jnp.exp2(m[...] - top)
    total = jnp.sum(l[...] * weight, axis=0, keepdims=True)
    lse[...] = top + jnp.log2(total)
    dl[...] = jnp.sum(d[...] * weight, axis=0, keepdims=True) / total

    def grads_unit(zp, h, slot):
        rows = pl.ds(pl.multiple_of(zp * 256, 256), 256)
        k_t = kv[2 * h, rows, :].T
        dk = jnp.zeros((256, LANES), F32)
        dv = jnp.zeros((256, LANES), F32)
        for tile in range((NQ - h * NP) // GW):
            there = pl.ds(tile * GW, GW)
            cs = pl.ds(h * NP + tile * GW, GW)
            p = jnp.exp2(stored[h][0][rows, there] - lse[:, cs])
            ds = (p * (stored[h][1][rows, there] - dl[:, cs]) * SCALE).astype(BF)
            dk += dot(ds, q[cs, :])
            dv += dot(p.astype(BF), do[cs, :])
            dq_t[:, cs] += dot(k_t, ds)
        for i, part in ((0, dk), (1, dv)):
            acc[slot, h, 0, i] = part[:128]
            acc[slot, h, 1, i] = part[128:]

    def sib_copy(t, h):
        return pltpu.make_async_remote_copy(
            src_ref=sib_out.at[t, h], dst_ref=sib_in.at[t, h], send_sem=rs_sib_send,
            recv_sem=rs_sib_recv.at[t, h], device_id={"blk": sib}, device_id_type=MESH,
        )

    def left_copy(k, h, i):
        return pltpu.make_async_remote_copy(
            src_ref=ring_out.at[k - 1, h, i], dst_ref=l_in.at[k - 1, h, i],
            send_sem=rs_send, recv_sem=l_recv.at[k - 1, h, i],
            device_id={"blk": left}, device_id_type=MESH,
        )

    def right_copy(k, h, i):
        return pltpu.make_async_remote_copy(
            src_ref=ring_out.at[k + 2, h, i], dst_ref=r_in.at[k - 1, h, i],
            send_sem=rs_send, recv_sem=r_recv.at[k - 1, h, i],
            device_id={"blk": right}, device_id_type=MESH,
        )

    def far_copy(h, i):
        return pltpu.make_async_remote_copy(
            src_ref=ring_out.at[6, h, i], dst_ref=far_in.at[h, i],
            send_sem=rs_send, recv_sem=far_recv.at[h, i],
            device_id={"blk": (left2, right2)[h]}, device_id_type=MESH,
        )

    def compute(t, h):
        k = jnp.where(t == 0, 4, 3 - (t - 1) // 2)
        zp = lax.rem(jnp.where(t % 2 == 1, z + 8 - k, z + k), 8)
        slot = t % 2
        if h == 0:
            grads_unit(zp, 0, slot)
        else:
            @pl.when(zp <= z)
            def _():
                grads_unit(zp, 1, slot)

            @pl.when(zp > z)
            def _():
                acc[slot, 1] = jnp.zeros(acc.shape[2:], F32)

        sib_out[t, h] = acc[slot, h, 1 - c].astype(BF)
        sib_copy(t, h).start()

    def finalize(t, h):
        k = 3 - (t - 1) // 2
        slot = t % 2
        sib_copy(t, h).wait_recv()
        for i in range(2):
            acc[slot, h, c, i] = acc[slot, h, c, i] + sib_in[t, h, i].astype(F32)

        def pass_on(place_of, copy_of, into, with_far):
            for i in range(2):
                @pl.when(k < 3)
                def _():
                    copy_of(k + 1, h, i).wait_recv()
                    acc[slot, h, c, i] = acc[slot, h, c, i] + into[k, h, i].astype(F32)

                if with_far:
                    @pl.when(k == 2)
                    def _():
                        far_copy(h, i).wait_recv()
                        acc[slot, h, c, i] = acc[slot, h, c, i] + far_in[h, i].astype(F32)

                ring_out[place_of, h, i] = acc[slot, h, c, i].astype(BF)
                copy_of(k, h, i).start()

        @pl.when(t == 0)
        def _():
            for i in range(2):
                ring_out[6, h, i] = acc[slot, h, c, i].astype(BF)
                far_copy(h, i).start()

        @pl.when(t % 2 == 1)
        def _():
            pass_on(k - 1, left_copy, l_in, h == 0)

        @pl.when((t % 2 == 0) & (t > 0))
        def _():
            pass_on(k + 2, right_copy, r_in, h == 1)

    def grads_step(t, carry):
        for h in range(2):
            compute(t, h)

            @pl.when(t > 0)
            def _():
                finalize(t - 1, h)

        return carry

    lax.fori_loop(0, 8, grads_step, 0)

    def peer(k, other):
        where = {"head": lax.rem(head + k, 8)}
        if other:
            where["pair"] = 1 - pair
        return where

    def to_heads(k, src, dst, send_sem, recv_sem, other=False):
        return pltpu.make_async_remote_copy(
            src_ref=src, dst_ref=dst, send_sem=send_sem, recv_sem=recv_sem,
            device_id=peer(k, other), device_id_type=MESH,
        )

    def dq_copies(k):
        h = lax.rem(head + k, 8)
        rows_p = dq.at[pl.ds(pl.multiple_of(h * 64, 64), 64), :]
        rows_r = dq.at[pl.ds(pl.multiple_of(NP + h * 128, 128), 128), :]
        return ((rows_p, o_dqp.at[head]), (rows_r, o_dqr.at[head]))

    def kv_rows(k):
        return pl.ds(pl.multiple_of(lax.rem(head + k, 8) * 16, 16), 16)

    dq[...] = dq_t[...].T.astype(BF)
    local = []
    for k in range(1, 8):
        for i, (src, dst) in enumerate(dq_copies(k)):
            to_heads(k, src, dst, end_send.at[i], end_recv.at[i]).start()
    for i, (src, dst) in enumerate(dq_copies(0)):
        copy = pltpu.make_async_copy(src, dst, loc_sem.at[i])
        copy.start()
        local.append(copy)

    for h in range(2):
        sib_copy(7, h).wait_recv()
        for i in range(2):
            part = acc[1, h, c, i] + sib_in[7, h, i].astype(F32)
            left_copy(1, h, i).wait_recv()
            right_copy(1, h, i).wait_recv()
            part = part + l_in[0, h, i].astype(F32) + r_in[0, h, i].astype(F32)
            fin[h, i] = part.astype(BF)
    for k in range(8):
        to_heads(
            k, fin.at[0, :, kv_rows(k), :], o_other.at[head], end_send.at[3], end_recv.at[3], other=True
        ).start()
    for k in range(1, 8):
        to_heads(
            k, fin.at[:, :, kv_rows(k), :], o_own.at[head], end_send.at[2], end_recv.at[2]
        ).start()
    copy = pltpu.make_async_copy(fin.at[:, :, kv_rows(0), :], o_own.at[head], loc_sem.at[2])
    copy.start()
    local.append(copy)

    def wait_sends(ref, sem):
        pltpu.make_async_copy(ref, ref, sem).wait()

    wait_sends(kv.at[:, pl.ds(0, 7 * 128), :], ag_ring_send)
    wait_sends(kv.at[:, pl.ds(0, 8 * 128), :], ag_sib_send)
    wait_sends(sib_out, rs_sib_send)
    wait_sends(ring_out, rs_send)
    wait_sends(dq.at[pl.ds(0, 7 * 64), :], end_send.at[0])
    wait_sends(dq.at[pl.ds(0, 7 * 128), :], end_send.at[1])
    wait_sends(fin.at[:, :, pl.ds(0, 7 * 16), :], end_send.at[2])
    wait_sends(fin.at[0], end_send.at[3])
    for copy in local:
        copy.wait()
    for sem, ref in enumerate((o_dqp, o_dqr, o_own)):
        wait_sends(ref.at[pl.ds(0, 7)], end_recv.at[sem])
    wait_sends(o_other, end_recv.at[3])


def place(
    i_dqp, i_dqr, i_own, i_other, o_pq, o_pk, o_pv, o_rq, o_rk, o_rv,
    dqp, dqr, own, other, b_pq, b_rq, b_kv, in_sems, sems,
):
    loads = [
        pltpu.make_async_copy(src, dst, in_sems.at[i])
        for i, (src, dst) in enumerate(((i_dqp, dqp), (i_dqr, dqr), (i_own, own), (i_other, other)))
    ]
    for load in loads:
        load.start()
    copies = []

    def send(i, src, dst):
        copy = pltpu.make_async_copy(src, dst, sems.at[i])
        copy.start()
        copies.append(copy)

    loads[1].wait()
    for g in range(8):
        b_rq[:, g] = dqr[g]
    send(0, b_rq, o_rq)
    loads[0].wait()
    for g in range(8):
        b_pq[:, g] = dqp[g]
    send(1, b_pq, o_pq)
    to = lax.broadcasted_iota(I32, (128, 128), 0)
    source = lax.broadcasted_iota(I32, (128, 128), 1)
    move = jnp.where(source == (to % 8) * 16 + to // 8, 1.0, 0.0).astype(BF)
    loads[2].wait()
    loads[3].wait()
    for i, out in enumerate((o_pk, o_pv, o_rk, o_rv)):
        rows = dot(move, own[:, i // 2, i % 2].reshape(128, LANES))
        if i < 2:
            rows = rows + dot(move, other[:, i].reshape(128, LANES))
        b_kv[i] = rows.astype(BF)
        send(2 + i, b_kv.at[i], out)
    for copy in copies:
        copy.wait()


def on_device(
    prefix_query_rows,
    prefix_key_rows,
    prefix_value_rows,
    prefix_output_gradient,
    resp_q,
    resp_k,
    response_value_rows,
    response_output_gradient,
    lengths,
    prefix_order,
):
    vm = pltpu.VMEM
    dma = pltpu.SemaphoreType.DMA
    out = jax.ShapeDtypeStruct
    dqp, dqr, own, other = pl.pallas_call(
        kernel,
        out_shape=(
            out((8, 64, LANES), BF),
            out((8, 128, LANES), BF),
            out((8, 2, 2, 16, LANES), BF),
            out((8, 2, 16, LANES), BF),
        ),
        in_specs=[pl.BlockSpec(memory_space=pltpu.HBM)] * 10,
        out_specs=[pl.BlockSpec(memory_space=pl.ANY)] * 4,
        scratch_shapes=[
            pltpu.SMEM((16,), I32),
            pltpu.SMEM((2,), I32),
            vm((4, 2048, LANES), BF),
            vm((NQ, LANES), BF),
            vm((NQ, LANES), BF),
            vm((LANES, NQ), BF),
            vm((LANES, NQ), BF),
            vm((8, NQ), F32),
            vm((8, NQ), F32),
            vm((8, NQ), F32),
            vm((1, NQ), F32),
            vm((1, NQ), F32),
            vm((LANES, NQ), F32),
            vm((128, TW), I32),
            vm((128, TW), I32),
            vm((2048, NQ), F32),
            vm((2048, NQ), F32),
            vm((2048, NR), F32),
            vm((2048, NR), F32),
            vm((2, 2, 2, 2, 128, LANES), F32),
            vm((8, 2, 2, 128, LANES), BF),
            vm((8, 2, 2, 128, LANES), BF),
            vm((7, 2, 2, 128, LANES), BF),
            vm((3, 2, 2, 128, LANES), BF),
            vm((3, 2, 2, 128, LANES), BF),
            vm((2, 2, 128, LANES), BF),
            vm((2, 2, 128, LANES), BF),
            vm((NQ, LANES), BF),
            dma((10,)),
            dma((4, 16)),
            dma,
            dma,
            dma,
            dma((8, 2)),
            dma,
            dma((3, 2, 2)),
            dma((3, 2, 2)),
            dma((2, 2)),
            dma((4,)),
            dma((4,)),
            dma((3,)),
        ],
        compiler_params=pltpu.CompilerParams(
            collective_id=0, has_side_effects=True, vmem_limit_bytes=56 << 20
        ),
    )(
        prefix_order,
        lengths,
        prefix_query_rows.reshape(NP, LANES),
        prefix_output_gradient.reshape(NP, LANES),
        resp_q.reshape(NR, LANES),
        response_output_gradient.reshape(NR, LANES),
        prefix_key_rows.reshape(128, LANES),
        prefix_value_rows.reshape(128, LANES),
        resp_k.reshape(128, LANES),
        response_value_rows.reshape(128, LANES),
    )
    any_space = pl.BlockSpec(memory_space=pl.ANY)
    return pl.pallas_call(
        place,
        out_shape=(
            out((16, 8, 4, LANES), BF),
            out((128, LANES), BF),
            out((128, LANES), BF),
            out((16, 8, 8, LANES), BF),
            out((128, LANES), BF),
            out((128, LANES), BF),
        ),
        in_specs=[any_space] * 4,
        out_specs=[any_space] * 6,
        scratch_shapes=[
            vm((8, 16, 4, LANES), BF),
            vm((8, 16, 8, LANES), BF),
            vm((8, 2, 2, 16, LANES), BF),
            vm((8, 2, 16, LANES), BF),
            vm((16, 8, 4, LANES), BF),
            vm((16, 8, 8, LANES), BF),
            vm((4, 128, LANES), BF),
            dma((4,)),
            dma((6,)),
        ],
    )(
        dqp.reshape(8, 16, 4, LANES),
        dqr.reshape(8, 16, 8, LANES),
        own,
        other,
    )


def shaped(*args):
    pq, pk, pv, rq, rk, rv = on_device(*args)
    keys = (16, 8, LANES)
    return (
        pq, pk.reshape(keys), pv.reshape(keys),
        rq[None], rk.reshape(keys)[None], rv.reshape(keys)[None],
    )


def solution(mesh):
    in_specs = (
        P("blk", "head", "pair", None),
        P("blk", "head", None),
        P("blk", "head", None),
        P("blk", "head", "pair", None),
        P("pair", "blk", "head", None, None),
        P("pair", "blk", "head", None),
        P("pair", "blk", "head", None),
        P("pair", "blk", "head", None, None),
        P(),
        P(),
    )
    out_specs = (
        P(("blk", "head"), None, "pair", None),
        P(("blk", "head"), None, None),
        P(("blk", "head"), None, None),
        P("pair", ("blk", "head"), None, None, None),
        P("pair", ("blk", "head"), None, None),
        P("pair", ("blk", "head"), None, None),
    )
    return jax.shard_map(
        shaped, mesh=mesh, in_specs=in_specs, out_specs=out_specs, check_vma=False
    )
```

time: 59.9 us -> 58.4 us (0.975)
  Pallas kernels: 59.1 us -> 57.6 us
    pallas_call x1, Pallas kernels: 57.1 us -> 55.6 us  [on_device(): pl.pallas_call(kernel, out_shape=(out((8, 64, LANES), BF), out((8, 128, L...]
where the time goes in v2:
time: 58.4 us; the launch traced here: 58.3 us
  Pallas kernels  57.6 us (99%)
  between operations  0.64 us (1%)
    pallas_call x1, Pallas kernels, on_device(): pl.pallas_call(kernel, out_shape=(out((8, 64, LANES), BF), out((8, 128, L...  55.6 us
    pallas_call x1, Pallas kernels, on_device(): pl.pallas_call(place, out_shape=(out((16, 8, 4, LANES), BF), out((128, LA...  2.07 us

profile of v2, /device:TPU:1, one launch (start us, length us, event | category | flops | bytes accessed | tf_op | source)
XLA Modules:
  0.0 58.3 jit_solution(5370166466652953229)
XLA Ops:
  0.6 55.6 %shard_map.145 = (bf16[8,64,128]{2,1,0:T(8,128)(2,1)}, bf16[8,128,128]{2,1,0:T(8,128)(2,1)}, bf16[8,2,2,16,128]{4,3,2,1,0:T(8,128)(2,1)}, bf16[8,2,16,128]{3,2,1,0:T(8,128)(2,1)}) custom-call(s32[16]{0:T(128)} %order_in.1, s32[2]{0:T(128)} %lengths_in.1, bf16[512,128]{1,0:T(8,128)(2,1)} %bitcast.18, bf16[512,128]{1,0:T(8,128)(2,1)} %bitcast.19, ...), custom_call_target="tpu_custom_call" | custom-call | tf_op jit(solution)/shard_map/pallas_call | solution.py:443
  56.2 2.1 %shard_map.146 = (bf16[16,8,4,128]{3,2,1,0:T(4,128)(2,1)}, bf16[128,128]{1,0:T(8,128)(2,1)}, bf16[128,128]{1,0:T(8,128)(2,1)}, bf16[16,8,8,128]{3,2,1,0:T(8,128)...) custom-call(bf16[8,16,4,128]{3,2,1,0:T(4,128)(2,1)} %bitcast.20, bf16[8,16,8,128]{3,2,1,0:T(8,128)(2,1)} %bitcast.15, ...), custom_call_target="tpu_custom_call" | custom-call | tf_op jit(solution)/shard_map/pallas_call | solution.py:512

commit v3 on v2

--- a/solution.py
+++ b/solution.py
@@ -39,7 +39,7 @@
     order, lengths,
     kv, q, do, q_t, do_t, m, l, d, lse, dl, dq_t, diff_p, diff_r,
     s_pre, dp_pre, s_res, dp_res,
-    acc, sib_out, sib_in, ring_out, l_in, r_in, far_in, fin, dq,
+    acc, sib_out, sib_in, ring_out, l_in, r_in, far_in, fin,
     in_sem, ag_recv, ag_ring_send, ag_sib_send,
     rs_sib_send, rs_sib_recv, rs_send, l_recv, r_recv, far_recv,
     end_send, end_recv, loc_sem,
@@ -89,7 +89,7 @@
         copy.start()
 
     def kv_copy(i, block, send_sem, target):
-        piece = kv.at[i, rows_of(block), :]
+        piece = kv.at[pl.ds(2 * i, 2), rows_of(block), :]
         return pltpu.make_async_remote_copy(
             src_ref=piece, dst_ref=piece, send_sem=send_sem, recv_sem=ag_recv.at[i, block],
             device_id={"blk": target}, device_id_type=MESH,
@@ -98,7 +98,7 @@
     for copy in loads[:4]:
         copy.wait()
     pl.semaphore_wait(barrier, 20)
-    for i in range(4):
+    for i in range(2):
         kv_copy(i, b, ag_ring_send, right).start()
         kv_copy(i, b, ag_ring_send, left).start()
         kv_copy(i, b, ag_sib_send, sib).start()
@@ -169,8 +169,8 @@
 
             kv_copy(i, block, ag_sib_send, sib).start()
 
-        for i in range(4):
-            there = i < 2
+        for i in range(2):
+            there = i == 0
 
             @pl.when((k < 4) | there)
             def _():
@@ -187,7 +187,7 @@
 
         k = (n + 1) // 2
         zp = lax.rem(jnp.where(n % 2 == 1, z + 8 - k, z + k), 8)
-        for i in range(4):
+        for i in range(2):
             kv_copy(i, 2 * zp + 1 - c, ag_sib_send, sib).wait_recv()
         totals_unit(zp, 0)
 
@@ -228,24 +228,24 @@
             recv_sem=rs_sib_recv.at[t, h], device_id={"blk": sib}, device_id_type=MESH,
         )
 
-    def left_copy(k, h, i):
+    def left_copy(k, h):
         return pltpu.make_async_remote_copy(
-            src_ref=ring_out.at[k - 1, h, i], dst_ref=l_in.at[k - 1, h, i],
-            send_sem=rs_send, recv_sem=l_recv.at[k - 1, h, i],
+            src_ref=ring_out.at[k - 1, h], dst_ref=l_in.at[k - 1, h],
+            send_sem=rs_send, recv_sem=l_recv.at[k - 1, h],
             device_id={"blk": left}, device_id_type=MESH,
         )
 
-    def right_copy(k, h, i):
+    def right_copy(k, h):
         return pltpu.make_async_remote_copy(
-            src_ref=ring_out.at[k + 2, h, i], dst_ref=r_in.at[k - 1, h, i],
-            send_sem=rs_send, recv_sem=r_recv.at[k - 1, h, i],
+            src_ref=ring_out.at[k + 2, h], dst_ref=r_in.at[k - 1, h],
+            send_sem=rs_send, recv_sem=r_recv.at[k - 1, h],
             device_id={"blk": right}, device_id_type=MESH,
         )
 
-    def far_copy(h, i):
+    def far_copy(h):
         return pltpu.make_async_remote_copy(
-            src_ref=ring_out.at[6, h, i], dst_ref=far_in.at[h, i],
-            send_sem=rs_send, recv_sem=far_recv.at[h, i],
+            src_ref=ring_out.at[6, h], dst_ref=far_in.at[h],
+            send_sem=rs_send, recv_sem=far_recv.at[h],
             device_id={"blk": (left2, right2)[h]}, device_id_type=MESH,
         )
 
@@ -271,30 +271,31 @@
         k = 3 - (t - 1) // 2
         slot = t % 2
         sib_copy(t, h).wait_recv()
-        for i in range(2):
-            acc[slot, h, c, i] = acc[slot, h, c, i] + sib_in[t, h, i].astype(F32)
+        part = acc[slot, h, c] + sib_in[t, h].astype(F32)
 
         def pass_on(place_of, copy_of, into, with_far):
-            for i in range(2):
-                @pl.when(k < 3)
-                def _():
-                    copy_of(k + 1, h, i).wait_recv()
-                    acc[slot, h, c, i] = acc[slot, h, c, i] + into[k, h, i].astype(F32)
-
+            @pl.when(k == 3)
+            def _():
+                ring_out[place_of, h] = part.astype(BF)
+
+            @pl.when(k < 3)
+            def _():
+                copy_of(k + 1, h).wait_recv()
+                acc[slot, h, c] = part + into[k, h].astype(F32)
                 if with_far:
                     @pl.when(k == 2)
                     def _():
-                        far_copy(h, i).wait_recv()
-                        acc[slot, h, c, i] = acc[slot, h, c, i] + far_in[h, i].astype(F32)
-
-                ring_out[place_of, h, i] = acc[slot, h, c, i].astype(BF)
-                copy_of(k, h, i).start()
+                        far_copy(h).wait_recv()
+                        acc[slot, h, c] = acc[slot, h, c] + far_in[h].astype(F32)
+
+                ring_out[place_of, h] = acc[slot, h, c].astype(BF)
+
+            copy_of(k, h).start()
 
         @pl.when(t == 0)
         def _():
-            for i in range(2):
-                ring_out[6, h, i] = acc[slot, h, c, i].astype(BF)
-                far_copy(h, i).start()
+            ring_out[6, h] = part.astype(BF)
+            far_copy(h).start()
 
         @pl.when(t % 2 == 1)
         def _():
@@ -330,14 +331,14 @@
 
     def dq_copies(k):
         h = lax.rem(head + k, 8)
-        rows_p = dq.at[pl.ds(pl.multiple_of(h * 64, 64), 64), :]
-        rows_r = dq.at[pl.ds(pl.multiple_of(NP + h * 128, 128), 128), :]
+        rows_p = q.at[pl.ds(pl.multiple_of(h * 64, 64), 64), :]
+        rows_r = q.at[pl.ds(pl.multiple_of(NP + h * 128, 128), 128), :]
         return ((rows_p, o_dqp.at[head]), (rows_r, o_dqr.at[head]))
 
     def kv_rows(k):
         return pl.ds(pl.multiple_of(lax.rem(head + k, 8) * 16, 16), 16)
 
-    dq[...] = dq_t[...].T.astype(BF)
+    q[...] = dq_t[...].T.astype(BF)
     local = []
     for k in range(1, 8):
         for i, (src, dst) in enumerate(dq_copies(k)):
@@ -349,20 +350,20 @@
 
     for h in range(2):
         sib_copy(7, h).wait_recv()
-        for i in range(2):
-            part = acc[1, h, c, i] + sib_in[7, h, i].astype(F32)
-            left_copy(1, h, i).wait_recv()
-            right_copy(1, h, i).wait_recv()
-            part = part + l_in[0, h, i].astype(F32) + r_in[0, h, i].astype(F32)
-            fin[h, i] = part.astype(BF)
-    for k in range(8):
-        to_heads(
-            k, fin.at[0, :, kv_rows(k), :], o_other.at[head], end_send.at[3], end_recv.at[3], other=True
-        ).start()
-    for k in range(1, 8):
-        to_heads(
-            k, fin.at[:, :, kv_rows(k), :], o_own.at[head], end_send.at[2], end_recv.at[2]
-        ).start()
+        part = acc[1, h, c] + sib_in[7, h].astype(F32)
+        left_copy(1, h).wait_recv()
+        right_copy(1, h).wait_recv()
+        fin[h] = (part + l_in[0, h].astype(F32) + r_in[0, h].astype(F32)).astype(BF)
+        if h == 0:
+            for k in range(8):
+                to_heads(
+                    k, fin.at[0, :, kv_rows(k), :], o_other.at[head], end_send.at[3],
+                    end_recv.at[3], other=True,
+                ).start()
+        for k in range(1, 8):
+            to_heads(
+                k, fin.at[h, :, kv_rows(k), :], o_own.at[head, h], end_send.at[2], end_recv.at[2]
+            ).start()
     copy = pltpu.make_async_copy(fin.at[:, :, kv_rows(0), :], o_own.at[head], loc_sem.at[2])
     copy.start()
     local.append(copy)
@@ -374,8 +375,8 @@
     wait_sends(kv.at[:, pl.ds(0, 8 * 128), :], ag_sib_send)
     wait_sends(sib_out, rs_sib_send)
     wait_sends(ring_out, rs_send)
-    wait_sends(dq.at[pl.ds(0, 7 * 64), :], end_send.at[0])
-    wait_sends(dq.at[pl.ds(0, 7 * 128), :], end_send.at[1])
+    wait_sends(q.at[pl.ds(0, 7 * 64), :], end_send.at[0])
+    wait_sends(q.at[pl.ds(0, 7 * 128), :], end_send.at[1])
     wait_sends(fin.at[:, :, pl.ds(0, 7 * 16), :], end_send.at[2])
     wait_sends(fin.at[0], end_send.at[3])
     for copy in local:
@@ -478,23 +479,22 @@
             vm((3, 2, 2, 128, LANES), BF),
             vm((2, 2, 128, LANES), BF),
             vm((2, 2, 128, LANES), BF),
-            vm((NQ, LANES), BF),
             dma((10,)),
-            dma((4, 16)),
+            dma((2, 16)),
             dma,
             dma,
             dma,
             dma((8, 2)),
             dma,
-            dma((3, 2, 2)),
-            dma((3, 2, 2)),
-            dma((2, 2)),
+            dma((3, 2)),
+            dma((3, 2)),
+            dma((2,)),
             dma((4,)),
             dma((4,)),
             dma((3,)),
         ],
         compiler_params=pltpu.CompilerParams(
-            collective_id=0, has_side_effects=True, vmem_limit_bytes=56 << 20
+            collective_id=0, has_side_effects=True, vmem_limit_bytes=52 << 20
         ),
     )(
         prefix_order,

time: 58.4 us -> 68.2 us (1.17)
  local copies, waits for them, and re-layouts: 0 us -> 9.98 us
    unnamed x0 -> x28, local copies, waits for them, and re-layouts: none -> 9.98 us
where the time goes in v3:
time: 68.2 us; the launch traced here: 67.7 us
  Pallas kernels  57 us (84%)
  local copies, waits for them, and re-layouts  9.98 us (15%)
    pallas_call x1, Pallas kernels, on_device(): pl.pallas_call(kernel, out_shape=(out((8, 64, LANES), BF), out((8, 128, L...  55 us
    unnamed x28, local copies, waits for them, and re-layouts  9.98 us
    pallas_call x1, Pallas kernels, on_device(): pl.pallas_call(place, out_shape=(out((16, 8, 4, LANES), BF), out((128, LA...  2.06 us

profile of v3, /device:TPU:1, one launch (start us, length us, event | category | flops | bytes accessed | tf_op | source)
XLA Modules:
  0.0 67.7 jit_solution(4358675690101194234)
XLA Ops:
  0.6 0.0 copy-start.12
  0.6 0.0 copy-start.13
  0.7 0.6 copy-done.12
  1.3 0.0 copy-done.13
  1.3 0.0 copy-start.1
  1.3 0.9 %copy-done.1 = bf16[1,128,1,8,128]{4,3,2,1,0:T(8,128)(2,1)S(1)} copy-done((bf16[1,128,1,8,128]{4,3,2,1,0:T(8,128)(2,1)S(1)}, bf16[1,128,1,8,128]{4,3,2,1,0:T(8,128)(2,1)}, u32[]{:S(2)}) %copy-start.1) | copy-done | bytes 262168
  2.3 0.0 copy-start.2
  2.3 0.9 %copy-done.2 = bf16[1,128,1,8,128]{4,3,2,1,0:T(8,128)(2,1)S(1)} copy-done((bf16[1,128,1,8,128]{4,3,2,1,0:T(8,128)(2,1)S(1)}, bf16[1,128,1,8,128]{4,3,2,1,0:T(8,128)(2,1)}, u32[]{:S(2)}) %copy-start.2) | copy-done | bytes 262168
  3.2 0.0 copy-start.3
  3.2 0.9 %copy-done.3 = bf16[128,1,4,128]{3,2,1,0:T(4,128)(2,1)S(1)} copy-done((bf16[128,1,4,128]{3,2,1,0:T(4,128)(2,1)S(1)}, bf16[128,1,4,128]{3,2,1,0:T(4,128)(2,1)}, u32[]{:S(2)}) %copy-start.3) | copy-done | bytes 131096
  4.1 0.0 copy-start.4
  4.1 0.9 %copy-done.4 = bf16[128,1,4,128]{3,2,1,0:T(4,128)(2,1)S(1)} copy-done((bf16[128,1,4,128]{3,2,1,0:T(4,128)(2,1)S(1)}, bf16[128,1,4,128]{3,2,1,0:T(4,128)(2,1)}, u32[]{:S(2)}) %copy-start.4) | copy-done | bytes 131096
  5.0 0.0 copy-start.8
  5.0 0.8 %copy-done.8 = bf16[128,1,128]{2,0,1:T(8,128)(2,1)S(1)} copy-done((bf16[128,1,128]{2,0,1:T(8,128)(2,1)S(1)}, bf16[128,1,128]{2,0,1:T(8,128)(2,1)}, u32[]{:S(2)}) %copy-start.8) | copy-done | bytes 32792
  5.8 0.0 copy-start.9
  5.8 0.8 %copy-done.9 = bf16[128,1,128]{2,0,1:T(8,128)(2,1)S(1)} copy-done((bf16[128,1,128]{2,0,1:T(8,128)(2,1)S(1)}, bf16[128,1,128]{2,0,1:T(8,128)(2,1)}, u32[]{:S(2)}) %copy-start.9) | copy-done | bytes 32792
  6.5 0.0 copy-start.10
  6.5 0.8 %copy-done.10 = bf16[1,128,1,128]{3,1,2,0:T(8,128)(2,1)S(1)} copy-done((bf16[1,128,1,128]{3,1,2,0:T(8,128)(2,1)S(1)}, bf16[1,128,1,128]{3,1,2,0:T(8,128)(2,1)}, u32[]{:S(2)}) %copy-start.10) | copy-done | bytes 32792
  7.3 0.0 copy-start.11
  7.3 0.8 %copy-done.11 = bf16[1,128,1,128]{3,1,2,0:T(8,128)(2,1)S(1)} copy-done((bf16[1,128,1,128]{3,1,2,0:T(8,128)(2,1)S(1)}, bf16[1,128,1,128]{3,1,2,0:T(8,128)(2,1)}, u32[]{:S(2)}) %copy-start.11) | copy-done | bytes 32792
  8.1 55.0 %shard_map.145 = (bf16[8,64,128]{2,1,0:T(8,128)(2,1)S(1)}, bf16[8,128,128]{2,1,0:T(8,128)(2,1)S(1)}, bf16[8,2,2,16,128]{4,3,2,1,0:T(8,128)(2,1)S(1)}, bf16[8,2,16,128]{3,2,1,0:T(8,128)(2,1)S(1)}) custom-call(s32[16]{0:T(128)S(1)} %copy-done.12, s32[2]{0:T(128)S(1)} %copy-done.13, bf16[512,128]{1,0:T(8,128)(2,1)S(1)} %bitcast.18, ...), custom_call_target="tpu_custom_call" | custom-call | tf_op jit(solution)/shard_map/pallas_call | solution.py:444
  63.0 0.0 copy-start
  63.0 0.7 %copy-done = bf16[8,128,128]{2,1,0:T(8,128)(2,1)} copy-done((bf16[8,128,128]{2,1,0:T(8,128)(2,1)}, bf16[8,128,128]{2,1,0:T(8,128)(2,1)S(1)}, u32[]{:S(2)}) %copy-start) | copy-done | bytes 262168
  63.7 0.0 copy-start.5
  63.7 0.6 copy-done.5
  64.4 0.0 copy-start.6
  64.4 0.6 copy-done.6
  65.0 0.0 copy-start.7
  65.0 0.6 copy-done.7
  65.6 2.1 %shard_map.146 = (bf16[16,8,4,128]{3,2,1,0:T(4,128)(2,1)}, bf16[128,128]{1,0:T(8,128)(2,1)}, bf16[128,128]{1,0:T(8,128)(2,1)}, bf16[16,8,8,128]{3,2,1,0:T(8,128)...) custom-call(bf16[8,16,4,128]{3,2,1,0:T(4,128)(2,1)} %bitcast.20, bf16[8,16,8,128]{3,2,1,0:T(8,128)(2,1)} %bitcast.15, ...), custom_call_target="tpu_custom_call" | custom-call | tf_op jit(solution)/shard_map/pallas_call | solution.py:512
Async XLA Ops:
  0.6 0.7 copy-start.12
  0.6 0.7 copy-start.13
  1.3 0.9 %copy-start.1 = (bf16[1,128,1,8,128]{4,3,2,1,0:T(8,128)(2,1)S(1)}, bf16[1,128,1,8,128]{4,3,2,1,0:T(8,128)(2,1)}, u32[]{:S(2)}) copy-start(bf16[1,128,1,8,128]{4,3,2,1,0:T(8,128)(2,1)} %param.14) | copy-start | bytes 786436
  2.3 0.9 %copy-start.2 = (bf16[1,128,1,8,128]{4,3,2,1,0:T(8,128)(2,1)S(1)}, bf16[1,128,1,8,128]{4,3,2,1,0:T(8,128)(2,1)}, u32[]{:S(2)}) copy-start(bf16[1,128,1,8,128]{4,3,2,1,0:T(8,128)(2,1)} %param.17) | copy-start | bytes 786436
  3.2 0.9 %copy-start.3 = (bf16[128,1,4,128]{3,2,1,0:T(4,128)(2,1)S(1)}, bf16[128,1,4,128]{3,2,1,0:T(4,128)(2,1)}, u32[]{:S(2)}) copy-start(bf16[128,1,4,128]{3,2,1,0:T(4,128)(2,1)} %param.10) | copy-start | bytes 393220
  4.1 0.9 %copy-start.4 = (bf16[128,1,4,128]{3,2,1,0:T(4,128)(2,1)S(1)}, bf16[128,1,4,128]{3,2,1,0:T(4,128)(2,1)}, u32[]{:S(2)}) copy-start(bf16[128,1,4,128]{3,2,1,0:T(4,128)(2,1)} %param.13) | copy-start | bytes 393220
  5.0 0.8 %copy-start.8 = (bf16[128,1,128]{2,0,1:T(8,128)(2,1)S(1)}, bf16[128,1,128]{2,0,1:T(8,128)(2,1)}, u32[]{:S(2)}) copy-start(bf16[128,1,128]{2,0,1:T(8,128)(2,1)} %param.11) | copy-start | bytes 98308
  5.8 0.8 %copy-start.9 = (bf16[128,1,128]{2,0,1:T(8,128)(2,1)S(1)}, bf16[128,1,128]{2,0,1:T(8,128)(2,1)}, u32[]{:S(2)}) copy-start(bf16[128,1,128]{2,0,1:T(8,128)(2,1)} %param.12) | copy-start | bytes 98308
  6.5 0.8 %copy-start.10 = (bf16[1,128,1,128]{3,1,2,0:T(8,128)(2,1)S(1)}, bf16[1,128,1,128]{3,1,2,0:T(8,128)(2,1)}, u32[]{:S(2)}) copy-start(bf16[1,128,1,128]{3,1,2,0:T(8,128)(2,1)} %param.15) | copy-start | bytes 98308
  7.3 0.8 %copy-start.11 = (bf16[1,128,1,128]{3,1,2,0:T(8,128)(2,1)S(1)}, bf16[1,128,1,128]{3,1,2,0:T(8,128)(2,1)}, u32[]{:S(2)}) copy-start(bf16[1,128,1,128]{3,1,2,0:T(8,128)(2,1)} %param.16) | copy-start | bytes 98308
  63.0 0.7 %copy-start = (bf16[8,128,128]{2,1,0:T(8,128)(2,1)}, bf16[8,128,128]{2,1,0:T(8,128)(2,1)S(1)}, u32[]{:S(2)}) copy-start(bf16[8,128,128]{2,1,0:T(8,128)(2,1)S(1)} %get-tuple-element.17) | copy-start | bytes 786436
  63.7 0.7 copy-start.5
  64.4 0.6 copy-start.6
  65.0 0.6 copy-start.7

commit v4 on v2

--- a/solution.py
+++ b/solution.py
@@ -355,14 +355,16 @@
             right_copy(1, h, i).wait_recv()
             part = part + l_in[0, h, i].astype(F32) + r_in[0, h, i].astype(F32)
             fin[h, i] = part.astype(BF)
-    for k in range(8):
-        to_heads(
-            k, fin.at[0, :, kv_rows(k), :], o_other.at[head], end_send.at[3], end_recv.at[3], other=True
-        ).start()
-    for k in range(1, 8):
-        to_heads(
-            k, fin.at[:, :, kv_rows(k), :], o_own.at[head], end_send.at[2], end_recv.at[2]
-        ).start()
+        if h == 0:
+            for k in range(8):
+                to_heads(
+                    k, fin.at[0, :, kv_rows(k), :], o_other.at[head], end_send.at[3],
+                    end_recv.at[3], other=True,
+                ).start()
+        for k in range(1, 8):
+            to_heads(
+                k, fin.at[h, :, kv_rows(k), :], o_own.at[head, h], end_send.at[2], end_recv.at[2]
+            ).start()
     copy = pltpu.make_async_copy(fin.at[:, :, kv_rows(0), :], o_own.at[head], loc_sem.at[2])
     copy.start()
     local.append(copy)

time: 58.4 us -> 58.2 us (level)
  no operation moved by 1% of the time
where the time goes in v4:
time: 58.2 us; the launch traced here: 58.1 us
  Pallas kernels  57.4 us (99%)
  between operations  0.64 us (1%)
    pallas_call x1, Pallas kernels, on_device(): pl.pallas_call(kernel, out_shape=(out((8, 64, LANES), BF), out((8, 128, L...  55.4 us
    pallas_call x1, Pallas kernels, on_device(): pl.pallas_call(place, out_shape=(out((16, 8, 4, LANES), BF), out((128, LA...  2.06 us

profile of v4, /device:TPU:1, one launch (start us, length us, event | category | flops | bytes accessed | tf_op | source)
XLA Modules:
  0.0 58.1 jit_solution(16581129389252219405)
XLA Ops:
  0.6 55.4 %shard_map.145 = (bf16[8,64,128]{2,1,0:T(8,128)(2,1)}, bf16[8,128,128]{2,1,0:T(8,128)(2,1)}, bf16[8,2,2,16,128]{4,3,2,1,0:T(8,128)(2,1)}, bf16[8,2,16,128]{3,2,1,0:T(8,128)(2,1)}) custom-call(s32[16]{0:T(128)} %order_in.1, s32[2]{0:T(128)} %lengths_in.1, bf16[512,128]{1,0:T(8,128)(2,1)} %bitcast.18, bf16[512,128]{1,0:T(8,128)(2,1)} %bitcast.19, ...), custom_call_target="tpu_custom_call" | custom-call | tf_op jit(solution)/shard_map/pallas_call | solution.py:445
  56.0 2.1 %shard_map.146 = (bf16[16,8,4,128]{3,2,1,0:T(4,128)(2,1)}, bf16[128,128]{1,0:T(8,128)(2,1)}, bf16[128,128]{1,0:T(8,128)(2,1)}, bf16[16,8,8,128]{3,2,1,0:T(8,128)...) custom-call(bf16[8,16,4,128]{3,2,1,0:T(4,128)(2,1)} %bitcast.20, bf16[8,16,8,128]{3,2,1,0:T(8,128)(2,1)} %bitcast.15, ...), custom_call_target="tpu_custom_call" | custom-call | tf_op jit(solution)/shard_map/pallas_call | solution.py:514
